TPU v7x, 256 devices: a whole 4x4x8 slice. The times are simulated.
256 devices in a mesh: replica: 8 (over y, z_hi), fsdp: 32 (over z_lo, x, core).
Axes of the slice: x: 4, y: 4, z: 8 (z_hi: 2, z_lo: 4; z = z_hi * 4 + z_lo), core: 2. Of those that a mesh axis runs over, the one named last changes fastest.
Arguments:
- residual: bfloat16 [8, 8192, 4608], P('replica', 'fsdp'), may hold values from -6 to 6
- cotangent: bfloat16 [8, 8192, 1024], P('replica', 'fsdp'), may hold values from -6 to 6
- norm_gain: float32 [8, 4608], P('replica'), may hold values from -0.5 to 0.5
- master: float32 [8, 4608, 1024], P('replica', 'fsdp'), may hold values from -6 to 6
- first_moment: float32 [8, 4608, 1024], P('replica', 'fsdp'), may hold values from -6 to 6
- second_moment: float32 [8, 4608, 1024], P('replica', 'fsdp'), may hold values from 0.05 to 2
- anchor: float32 [4608, 1024], P('fsdp'), may hold values from -6 to 6
- outer_momentum: float32 [4608, 1024], P('fsdp'), may hold values from -4 to 4
- history: float32 [8, 4, 768, 1024], P('replica', None, 'fsdp'), may hold values from -6 to 6
- fragment: int32 [576], replicated, may hold values from 0 to 5, as said below
- delay: int32 [8, 96], P('replica', 'fsdp'), may hold values from 1 to 4
Outputs:
- values: bfloat16 [8, 8192, 1024], P('replica', 'fsdp')
- input_grad: bfloat16 [8, 8192, 4608], P('replica', 'fsdp')
- gain_grad: float32 [8, 4608], P('replica')
- new_master: float32 [8, 4608, 1024], P('replica', 'fsdp')
- new_first: float32 [8, 4608, 1024], P('replica', 'fsdp')
- new_second: float32 [8, 4608, 1024], P('replica', 'fsdp')
- new_anchor: float32 [4608, 1024], P('fsdp')
- new_momentum: float32 [4608, 1024], P('fsdp')
Inputs may be any that keep to these rules, and one draw needn't show every extreme that they name: Each aligned run of 6 row blocks (blocks 0 to 5, 6 to 11 and so on) holds every fragment number exactly once.
All inputs are finite; a program needn't handle non-finite values.
Results may differ from a plain program's by a relative error of at most 0.013.
Values may be sent and summed in bfloat16 or wider, within the bound.
A program may use at most 128 MiB of HBM per device.

v0:
```python
import jax
import jax.numpy as jnp
from jax import lax
from jax.sharding import PartitionSpec as P

D = 4608
FRAGS = 6
FR_ROWS = 8


norm_eps = 1e-06
beta_one = 0.9
beta_two = 0.95
inner_rate = 0.01
weight_decay = 0.1
adam_eps = 1e-08
outer_beta = 0.9
outer_rate = 0.7
mix_weight = 0.5


def local_blocks(fragment, local_rows):
    count = local_rows // FR_ROWS
    start = lax.axis_index("fsdp") * count
    owned = lax.dynamic_slice_in_dim(fragment, start, count, 0)
    order = jnp.argsort(jnp.where(owned == 0, 0, 1).astype(jnp.int32), stable=True)
    return order[: count // FRAGS]


def take_part(array, chosen):
    view = array.reshape(array.shape[0] // FR_ROWS, FR_ROWS, array.shape[1])
    return view[chosen].reshape(chosen.shape[0] * FR_ROWS, array.shape[1])


def put_part(array, part, chosen):
    view = array.reshape(array.shape[0] // FR_ROWS, FR_ROWS, array.shape[1])
    placed = view.at[chosen].set(part.reshape(chosen.shape[0], FR_ROWS, array.shape[1]))
    return placed.reshape(array.shape)


def pick_snapshot(stack, ages):
    blocks = stack.shape[1] // FR_ROWS
    view = stack.reshape(stack.shape[0], blocks, FR_ROWS, stack.shape[2])
    levels = jnp.arange(stack.shape[0], dtype=jnp.int32)
    mask = levels[:, None] == ages[None, :] - 1
    picked = jnp.sum(jnp.where(mask[:, :, None, None], view, jnp.zeros_like(view)), axis=0)
    return picked.reshape(stack.shape[1], stack.shape[2])


def nesterov(delta, momentum_old, anchor_old):
    momentum_new = outer_beta * momentum_old + delta
    anchor_new = anchor_old - outer_rate * (delta + outer_beta * momentum_new)
    return (anchor_new, momentum_new)


def outer_sync(anchor, outer_momentum, history, chosen, ages):
    replicas = lax.axis_size("replica")
    anchor_old = take_part(anchor, chosen)
    momentum_old = take_part(outer_momentum, chosen)
    snapshot = pick_snapshot(history[0], ages)
    term = anchor_old - snapshot
    delta = lax.psum(term.astype(jnp.bfloat16), "replica").astype(jnp.float32) / replicas
    return nesterov(delta, momentum_old, anchor_old)


def body(
    residual,
    cotangent,
    norm_gain,
    master,
    first_moment,
    second_moment,
    anchor,
    outer_momentum,
    history,
    fragment,
    delay,
):
    out_scale = float(D) ** (-0.5)
    weights_master = master[0]
    local_rows = weights_master.shape[0]
    chosen = local_blocks(fragment, local_rows)
    hidden_in = residual[0].astype(jnp.float32)
    inverse_rms = lax.rsqrt(jnp.mean(hidden_in * hidden_in, axis=1, keepdims=True) + norm_eps)
    unit_rows = hidden_in * inverse_rms
    gain_factor = 1.0 + norm_gain[0]
    normed = (unit_rows * gain_factor).astype(jnp.bfloat16)
    incoming = cotangent[0]
    weights_bf = weights_master.astype(jnp.bfloat16)
    piece = lax.all_gather(weights_bf, "fsdp", axis=0, tiled=True)
    columns = normed
    value_total = jnp.dot(columns, piece, preferred_element_type=jnp.float32)
    back_part = lax.dot_general(
        incoming, piece, (((1,), (1,)), ((), ())), preferred_element_type=jnp.float32
    )
    dnormed_total = back_part
    value_total, dnormed_total = (value_total, dnormed_total)
    values = (value_total * out_scale).astype(jnp.bfloat16)
    dnormed = dnormed_total * out_scale
    gain_total = lax.psum(jnp.sum(dnormed * unit_rows, axis=0), "fsdp")
    scaled_up = dnormed * gain_factor
    input_grad = (
        inverse_rms
        * (scaled_up - unit_rows * jnp.mean(scaled_up * unit_rows, axis=1, keepdims=True))
    ).astype(jnp.bfloat16)
    columns = normed
    gradient = lax.psum_scatter(
        (
            lax.dot_general(
                columns, incoming, (((0,), (0,)), ((), ())), preferred_element_type=jnp.float32
            )
            * out_scale
        ).astype(jnp.bfloat16),
        "fsdp",
        scatter_dimension=0,
        tiled=True,
    ).astype(jnp.float32)
    first_new = beta_one * first_moment[0] + (1.0 - beta_one) * gradient
    second_new = beta_two * second_moment[0] + (1.0 - beta_two) * gradient * gradient
    stepped = weights_master - inner_rate * (
        first_new / (jnp.sqrt(second_new) + adam_eps) + weight_decay * weights_master
    )
    anchor_part, momentum_part = outer_sync(anchor, outer_momentum, history, chosen, delay[0])
    new_anchor = put_part(anchor, anchor_part, chosen)
    new_momentum = put_part(outer_momentum, momentum_part, chosen)
    mixed = mix_weight * take_part(stepped, chosen) + (1.0 - mix_weight) * anchor_part
    new_master = put_part(stepped, mixed, chosen)
    return (
        values[None],
        input_grad[None],
        gain_total[None],
        new_master[None],
        first_new[None],
        second_new[None],
        new_anchor,
        new_momentum,
    )


def solution(mesh):
    return jax.shard_map(
        body,
        mesh=mesh,
        in_specs=(
            P("replica", "fsdp", None),
            P("replica", "fsdp", None),
            P("replica", None),
            P("replica", "fsdp", None),
            P("replica", "fsdp", None),
            P("replica", "fsdp", None),
            P("fsdp", None),
            P("fsdp", None),
            P("replica", None, "fsdp", None),
            P(),
            P("replica", "fsdp"),
        ),
        out_specs=(
            P("replica", "fsdp", None),
            P("replica", "fsdp", None),
            P("replica", None),
            P("replica", "fsdp", None),
            P("replica", "fsdp", None),
            P("replica", "fsdp", None),
            P("fsdp", None),
            P("fsdp", None),
        ),
        check_vma=False,
    )
```

profile of v0, /device:TPU:16, one launch (start us, length us, event | category | flops | bytes accessed | tf_op | source)
XLA Modules:
  0.0 264.2 jit_solution(17432075641473774296)
XLA Ops:
  7.2 0.0 copy-start
  7.2 0.0 copy-start.1
  7.2 0.0 all-gather.2.cloned.1.call-start
  7.2 1.2 copy.25
  8.5 0.0 copy-start.4
  8.5 2.1 copy.24
  10.6 1.8 bitcast_convert_fusion
  12.4 0.0 all-gather.2.cloned.1.call-update
  12.4 0.0 reduce-scatter.2.cloned.1.call-start
  12.5 0.8 add_reduce_fusion
  13.3 0.0 copy-done.1
  13.3 0.0 copy-start.7
  13.3 0.5 fusion.12
  13.8 0.0 copy-done.7
  13.9 0.0 copy-done
  13.9 5.3 %multiply_convert_fusion = bf16[4608,1024]{1,0:T(8,128)(2,1)} fusion(bf16[1,256,4608]{2,1,0:T(8,128)(2,1)S(1)} %copy-done.1, f32[4608]{0:T(1024)S(1)} %add_reduce_fusion, f32[256]{0:T(256)S(1)} %add_rsqrt_fusion, bf16[1,256,1024]{2,1,0:T(8,128)(2,1)S(1)} %copy-done), kind=kOutput, calls=%fused_computation.6 | convolution fusion | flops 2430074880 | bytes 12340224 | tf_op jit(solution)/shard_map/dot_general | solution.py:109
  19.2 0.0 copy-start.9
  19.2 0.0 reduce-scatter.2.cloned.1.call-update
  19.3 0.6 copy-done.9
  19.9 0.1 broadcast_in_dim.55
  20.0 0.1 broadcast_in_dim.56
  20.1 0.8 compare_select_fusion.1
  20.8 1.6 sort.17
  22.5 0.0 copy-done.4
  22.5 1.2 gather_fusion.2
  23.7 1.6 gather_fusion.1
  25.3 0.0 copy-start.6
  25.3 1.1 select_reduce_fusion
  26.5 54.2 %psum.15 = bf16[24,1024]{1,0:T(8,128)(2,1)S(1)} all-reduce(bf16[24,1024]{1,0:T(8,128)(2,1)S(1)} %fusion.43), channel_id=1, replica_groups=mesh['replica'=8,'fsdp'=32] {'replica'}, use_global_device_ids=true, to_apply=%region_7.8 | all-reduce | flops 24576 | bytes 98304 | tf_op jit(solution)/shard_map/psum | solution.py:62
  80.7 0.7 broadcast_multiply_fusion
  81.4 0.0 copy-start.8
  81.4 6.2 %all-gather.2.cloned.1.call-done = bf16[4608,1024]{1,0:T(8,128)(2,1)} async-done(((bf16[144,1024]{1,0:T(8,128)(2,1)}), bf16[4608,1024]{1,0:T(8,128)(2,1)}) %all-gather.2.cloned.1.call-update) | async-done | bytes 9437200 | tf_op jit(solution)/shard_map/all_gather | solution.py:90
  87.7 9.2 %fusion.11 = (f32[4608]{0:T(1024)S(1)}, f32[256]{0:T(256)S(1)}, f32[256,4608]{1,0:T(8,128)}) fusion(bf16[1,256,4608]{2,1,0:T(8,128)(2,1)S(1)} %copy-done.1, f32[256]{0:T(256)S(1)} %add_rsqrt_fusion, f32[4608]{0:T(1024)S(1)} %broadcast_multiply_fusion, bf16[4608,1024]{1,0:T(8,128)(2,1)} %all-gather.2.cloned.1.call-done, bf16[1,256,1024]{2,1,0:T(8,128)(2,1)S(1)} %copy-done), kind=kOutput, calls=%fused_computation.20 | convolution fusion | flops 2425351424 | bytes 17078272 | tf_op jit(solution)/shard_map/dot_general | solution.py:93
  96.8 0.0 copy-done.6
  96.9 136.3 %psum.14 = f32[1,4608]{1,0:T(1,128)} all-reduce(f32[1,4608]{1,0:T(1,128)S(1)} %broadcast_in_dim.52), channel_id=1, replica_groups=mesh['replica'=8,'fsdp'=32] {'fsdp'}, use_global_device_ids=true, to_apply=%region_3.4 | all-reduce | flops 4608 | bytes 36864 | tf_op jit(solution)/shard_map/psum | solution.py:100
  233.2 0.0 copy-done.8
  233.2 0.0 copy-start.2
  233.2 7.3 %fusion.30 = bf16[1,256,1024]{2,1,0:T(8,128)(2,1)} fusion(bf16[4608,1024]{1,0:T(8,128)(2,1)} %all-gather.2.cloned.1.call-done, bf16[1,256,4608]{2,1,0:T(8,128)(2,1)S(1)} %copy-done.1, f32[4608]{0:T(1024)S(1)} %copy-done.8, f32[256]{0:T(256)S(1)} %add_rsqrt_fusion), kind=kOutput, calls=%fused_computation.33 | convolution fusion | flops 2421161984 | bytes 12340224 | tf_op jit(solution)/shard_map/dot_general | solution.py:92
  240.5 0.0 copy-done.2
  240.5 0.0 copy-start.3
  240.5 2.8 %fusion.17 = bf16[1,256,4608]{2,1,0:T(8,128)(2,1)} fusion(bf16[1,256,4608]{2,1,0:T(8,128)(2,1)S(1)} %copy-done.1, f32[256,4608]{1,0:T(8,128)S(1)} %copy-done.2, f32[256]{0:T(256)S(1)} %broadcast_multiply_fusion.1, f32[4608]{0:T(1024)S(1)} %broadcast_multiply_fusion, f32[256]{0:T(256)S(1)} %add_rsqrt_fusion), kind=kLoop, calls=%fused_computation.25 | loop fusion | flops 8257536 | bytes 9457664 | tf_op jit(solution)/shard_map/broadcast_in_dim | solution.py:130
  243.2 5.2 %reduce-scatter.2.cloned.1.call-done = bf16[144,1024]{1,0:T(8,128)(2,1)} async-done(((bf16[4608,1024]{1,0:T(8,128)(2,1)}), bf16[144,1024]{1,0:T(8,128)(2,1)}) %reduce-scatter.2.cloned.1.call-update) | async-done | bytes 294928 | tf_op jit(solution)/shard_map/reduce_scatter | solution.py:107
  248.4 0.0 copy-done.3
  248.4 2.8 %fusion.42 = (f32[1,144,1024]{2,1,0:T(8,128)}, f32[18,8,1024]{2,1,0:T(8,128)S(1)}, f32[1,144,1024]{2,1,0:T(8,128)}) fusion(bf16[144,1024]{1,0:T(8,128)(2,1)} %reduce-scatter.2.cloned.1.call-done, f32[1,144,1024]{2,1,0:T(8,128)} %param.16, f32[1,144,1024]{2,1,0:T(8,128)} %param.15, f32[1,144,1024]{2,1,0:T(8,128)S(1)} %copy-done.3), kind=kLoop, calls=%fused_computation.49 | loop fusion | flops 2064384 | bytes 3833856 | tf_op jit(solution)/shard_map/broadcast_in_dim | solution.py:134
  251.2 0.6 gather_fusion
  251.7 1.0 fusion.47
  252.7 0.6 scatter_fusion
  253.4 0.0 copy-start.5
  253.4 2.0 scatter_fusion.1
  255.4 2.0 scatter_fusion.2
  257.4 0.0 copy-done.5
  (9 shorter events, 0.1 us)
Async XLA Ops:
  7.2 6.7 %copy-start = (bf16[1,256,1024]{2,1,0:T(8,128)(2,1)S(1)}, bf16[1,256,1024]{2,1,0:T(8,128)(2,1)}, u32[]{:S(2)}) copy-start(bf16[1,256,1024]{2,1,0:T(8,128)(2,1)} %param.12) | copy-start | bytes 1572868
  7.2 6.1 %copy-start.1 = (bf16[1,256,4608]{2,1,0:T(8,128)(2,1)S(1)}, bf16[1,256,4608]{2,1,0:T(8,128)(2,1)}, u32[]{:S(2)}) copy-start(bf16[1,256,4608]{2,1,0:T(8,128)(2,1)} %param.11) | copy-start | bytes 7077892
  7.2 80.5 %all-gather.2.cloned.1.call-start = ((), (), s32[]{:S(2)}) async-start(), calls=%async_computation.1 | async-start | bytes 9732096 | tf_op jit(solution)/shard_map/all_gather | solution.py:90
  8.5 14.0 %copy-start.4 = (f32[144,1024]{1,0:T(8,128)}, f32[144,1024]{1,0:T(8,128)S(1)}, u32[]{:S(2)}) copy-start(f32[144,1024]{1,0:T(8,128)S(1)} %copy.25) | copy-start | bytes 1769476
  12.4 236.0 %reduce-scatter.2.cloned.1.call-start = ((), (), s32[]{:S(2)}) async-start(), calls=%async_computation.2 | async-start | bytes 9732096 | tf_op jit(solution)/shard_map/reduce_scatter | solution.py:107
  13.3 0.6 copy-start.7
  19.2 0.7 copy-start.9
  25.3 71.6 %copy-start.6 = (f32[3,8,1024]{2,1,0:T(8,128)}, f32[3,8,1024]{2,1,0:T(8,128)S(1)}, u32[]{:S(2)}) copy-start(f32[3,8,1024]{2,1,0:T(8,128)S(1)} %gather_fusion.1) | copy-start | bytes 294916
  81.4 151.8 %copy-start.8 = (f32[4608]{0:T(1024)S(1)}, f32[4608]{0:T(1024)}, u32[]{:S(2)}) copy-start(f32[4608]{0:T(1024)} %copy-done.7) | copy-start | bytes 55300
  233.2 7.3 %copy-start.2 = (f32[256,4608]{1,0:T(8,128)S(1)}, f32[256,4608]{1,0:T(8,128)}, u32[]{:S(2)}) copy-start(f32[256,4608]{1,0:T(8,128)} %get-tuple-element.18) | copy-start | bytes 14155780
  240.5 7.9 %copy-start.3 = (f32[1,144,1024]{2,1,0:T(8,128)S(1)}, f32[1,144,1024]{2,1,0:T(8,128)}, u32[]{:S(2)}) copy-start(f32[1,144,1024]{2,1,0:T(8,128)} %param.14) | copy-start | bytes 1769476
  253.4 4.0 %copy-start.5 = (f32[18,8,1024]{2,1,0:T(8,128)}, f32[18,8,1024]{2,1,0:T(8,128)S(1)}, u32[]{:S(2)}) copy-start(f32[18,8,1024]{2,1,0:T(8,128)S(1)} %scatter_fusion) | copy-start | bytes 1769476
Sparse Core Ops, SparseCore 0:
  12.6 75.0 all-gather.1
  90.2 158.1 reduce-scatter.1
where the time goes:
time: 265 us; the launch traced here: 264 us
  blocking collectives  191 us (72%)
  matrix products  21.8 us (8%)
  between operations  14.2 us (5%)
  other arithmetic  13.9 us (5%)
  local copies, waits for them, and re-layouts  12.2 us (5%)
  waiting for transfers between devices  11.4 us (4%)
    psum x1, blocking collectives, body(): gain_total = lax.psum(jnp.sum(dnormed * unit_rows, axis=0), 'fsdp')  136 us
    psum x1, blocking collectives, outer_sync(): lax.psum(term.astype(jnp.bfloat16), 'replica').astype(jnp.float32)  54.2 us
    dot_general x1, matrix products, body(): lax.dot_general(incoming, piece, (((1,), (1,)), ((), ())), preferred_elem...  9.19 us
    dot_general x1, matrix products, body(): value_total = jnp.dot(columns, piece, preferred_element_type=jnp.float32)  7.28 us
    all_gather x1, waiting for transfers between devices, body(): piece = lax.all_gather(weights_bf, 'fsdp', axis=0, tiled=True)  6.22 us
    dot_general x1, matrix products, body(): lax.dot_general(columns, incoming, (((0,), (0,)), ((), ())), preferred_el...  5.34 us
  transfers between devices with their start and end apart: 2, of which 2 were waited for; matrix products, arithmetic and copies ran while one was open for 13% of the time, Pallas kernels for 0%

commit v1 on v0

v1 whole, which is shorter than its diff:
```python
import jax
import jax.numpy as jnp
from jax import lax
from jax.experimental import pallas as pl
from jax.experimental.pallas import tpu as pltpu
from jax.sharding import PartitionSpec as P

D = 4608
DV = 1024
FRAGS = 6
FR_ROWS = 8
HIST = 4

T = 256
R = 144
SLOT = 2 * R
ZR = 4 * SLOT
H = 2 * ZR
TILE = 384
NZ = 640
NX = DV - NZ
PART = R // FRAGS
QUART = DV // 4

norm_eps = 1e-06
beta_one = 0.9
beta_two = 0.95
inner_rate = 0.01
weight_decay = 0.1
adam_eps = 1e-08
outer_beta = 0.9
outer_rate = 0.7
mix_weight = 0.5
out_scale = float(D) ** (-0.5)

MESH = pl.DeviceIdType.MESH
F32 = jnp.float32
BF16 = jnp.bfloat16


def main_kernel(
    frag, delay, residual, cotangent, gain, master, anchor, history,
    values_o, igrad_o, ggrad_o, grad_o, delta_o,
    res, resp, cot, gain_v, master_v, anchor_v, hist_v,
    wh, stage, g, normed, inv, dn, vacc, vrecv, vout, rs, rsp, ig, ggx, ggz, ggt,
    opp, full, zbuf, zxbuf, oppx, fullx, oterm, obuf, osum, ozh, od,
    loc, part_s, part_r, agz_s, agz_r, agx_s, agx_r, axx_s, axx_r, axz_s, axz_r,
    rsx_s, rsx_r, rsz_s, rsz_r, rxz_s, rxz_r, rxx_s, rxx_r, gx_s, gx_r, gz_s, gz_r,
    oy_s, oy_r, oz_s, oz_r, ob_s, ob_r,
):
    me = lax.axis_index("fsdp")
    rep = lax.axis_index("replica")
    q, x, c = me // 8, (me // 2) % 4, me % 2
    y, zh = rep // 2, rep % 2
    xr, xl, xo = (x + 1) % 4, (x + 3) % 4, (x + 2) % 4
    handler = c == q // 2
    near = jnp.where(q <= 2 * c, 0, 1)
    far = 1 - near

    def dev(qq, xx, cc):
        return {"fsdp": qq * 8 + xx * 2 + cc}

    partner, right, left = dev(q, x, 1 - c), dev(q, xr, c), dev(q, xl, c)
    up, down = dev(q + 1, x, c), dev(q - 1, x, c)

    sends = []

    def copy(src, dst, send, recv, to):
        return pltpu.make_async_remote_copy(
            src_ref=src, dst_ref=dst, send_sem=send, recv_sem=recv, device_id=to, device_id_type=MESH
        )

    def when(cond, run):
        if cond is None:
            run()
        else:
            @pl.when(cond)
            def _():
                run()

    def go(src, dst, send, recv, to, cond=None):
        made = copy(src, dst, send, recv, to)
        when(cond, lambda: made.start())
        sends.append((cond, made))

    def got(dst, recv, cond=None):
        made = copy(dst, dst, part_s.at[0], recv, partner)
        when(cond, lambda: made.wait_recv())

    local_in = [
        pltpu.make_async_copy(master.at[0], master_v, loc.at[0]),
        pltpu.make_async_copy(residual.at[0], res, loc.at[1]),
        pltpu.make_async_copy(cotangent.at[0], cot.at[pl.ds(0, T)], loc.at[2]),
        pltpu.make_async_copy(gain, gain_v, loc.at[3]),
        pltpu.make_async_copy(anchor, anchor_v, loc.at[4]),
        pltpu.make_async_copy(history.at[0], hist_v, loc.at[5]),
    ]
    for item in local_in:
        item.start()

    barrier = pltpu.get_barrier_semaphore()
    greeted = [partner]
    greeted += [dev(q, (x + k) % 4, c) for k in range(1, 4)]
    greeted += [dev((q + k) % 4, x, c) for k in range(1, 4)]
    greeted += [{"replica": ((y + k) % 4) * 2 + zh} for k in range(1, 4)]
    greeted += [{"replica": y * 2 + 1 - zh}]
    for to in greeted:
        pl.semaphore_signal(barrier, inc=1, device_id=to, device_id_type=MESH)
    pl.semaphore_wait(barrier, len(greeted))

    zcols, xcols = pl.ds(0, NZ), pl.ds(NZ, NX)

    def rows(zl, xx, half=0):
        return pl.multiple_of(zl * ZR + xx * SLOT + half * R, 16)

    def block(buf, zl, xx, cols, half=None):
        if half is None:
            return buf.at[pl.ds(rows(zl, xx), SLOT), cols]
        return buf.at[pl.ds(rows(zl, xx, half), R), cols]

    hcol = pl.multiple_of(c * H, 128)
    pcol = pl.multiple_of((1 - c) * H, 128)

    go(residual.at[0, :, pl.ds(pcol, H)], resp, part_s.at[1], part_r.at[1], partner)
    go(cotangent.at[0], cot.at[pl.ds(T, T)], part_s.at[2], part_r.at[2], partner)

    own = q % 2
    local_in[0].wait()
    own_rows = pl.ds(pl.multiple_of(own * ZR + x * SLOT + c * R, 16), R)

    @pl.when(handler)
    def _():
        wh[own_rows, :] = master_v[...].astype(BF16)

    @pl.when(jnp.logical_not(handler))
    def _():
        stage[...] = master_v[...].astype(BF16)

    go(stage, wh.at[own_rows, :], part_s.at[0], part_r.at[0], partner, jnp.logical_not(handler))
    other_rows = pl.ds(pl.multiple_of(own * ZR + x * SLOT + (1 - c) * R, 16), R)
    got(wh.at[other_rows, :], part_r.at[0], handler)

    def ag_z(zl, cond_extra=None):
        target = 2 * c + zl
        ref = block(wh, zl, x, zcols)
        got(ref, agz_r.at[zl], q != target)
        go(ref, ref, agz_s.at[zl, 0], agz_r.at[zl], up, jnp.logical_and(q >= target, q < 3))
        go(ref, ref, agz_s.at[zl, 1], agz_r.at[zl], down, jnp.logical_and(q <= target, q > 0))

    def ag_x(zl):
        ref = block(wh, zl, x, zcols)
        go(ref, ref, agx_s.at[zl, 0], agx_r.at[zl, 0], right)
        go(ref, ref, agx_s.at[zl, 1], agx_r.at[zl, 1], left)

    def ag_fwd(zl):
        got(block(wh, zl, xl, zcols), agx_r.at[zl, 0])
        ref = block(wh, zl, xl, zcols, 0)
        go(ref, ref, agx_s.at[zl, 2], agx_r.at[zl, 2], right)
        got(block(wh, zl, xr, zcols), agx_r.at[zl, 1])
        ref = block(wh, zl, xr, zcols, 1)
        go(ref, ref, agx_s.at[zl, 3], agx_r.at[zl, 3], left)

    def ag_end(zl):
        got(block(wh, zl, xo, zcols, 0), agx_r.at[zl, 2])
        got(block(wh, zl, xo, zcols, 1), agx_r.at[zl, 3])

    def agx_zsend(zl, slots):
        target = 2 * c + zl
        for k in slots:
            xx = (x, xl, xr, xo)[k]
            ref = block(wh, zl, xx, xcols)
            got(ref, axz_r.at[zl, k], q != target)
            go(ref, ref, axz_s.at[zl, k, 0], axz_r.at[zl, k], up, jnp.logical_and(q >= target, q < 3))
            go(ref, ref, axz_s.at[zl, k, 1], axz_r.at[zl, k], down, jnp.logical_and(q <= target, q > 0))

    if NX:
        ref = block(wh, own, x, xcols)
        go(ref, ref, axx_s.at[0], axx_r.at[0], right, handler)
        go(ref, ref, axx_s.at[1], axx_r.at[1], left, handler)

    target = 2 * c + near
    ref = block(wh, near, x, zcols)
    go(ref, ref, agz_s.at[near, 0], agz_r.at[near], up, jnp.logical_and(handler, q < 3))
    go(ref, ref, agz_s.at[near, 1], agz_r.at[near], down, jnp.logical_and(handler, q > 0))

    def norm_rows(i, _):
        spot = pl.ds(pl.multiple_of(i * 16, 16), 16)
        raw = res[spot, :].astype(F32)
        scale = lax.rsqrt(jnp.mean(raw * raw, axis=1, keepdims=True) + norm_eps)
        inv[spot, :] = jnp.broadcast_to(scale, (16, 128))
        return 0

    local_in[1].wait()
    lax.fori_loop(0, T // 16, norm_rows, 0)
    inv_own = inv.at[pl.ds(0, T)]
    inv_other = inv.at[pl.ds(T, T)]
    go(inv_own, inv_other, part_s.at[3], part_r.at[3], partner)

    if NX:
        got(block(wh, own, xl, xcols), axx_r.at[0], handler)
        ref = block(wh, own, xl, xcols, 0)
        go(ref, ref, axx_s.at[2], axx_r.at[2], right, handler)
        got(block(wh, own, xr, xcols), axx_r.at[1], handler)
        ref = block(wh, own, xr, xcols, 1)
        go(ref, ref, axx_s.at[3], axx_r.at[3], left, handler)

        def agx_own(slots):
            for k in slots:
                xx = (x, xl, xr, xo)[k]
                ref = block(wh, near, xx, xcols)
                go(ref, ref, axz_s.at[near, k, 0], axz_r.at[near, k], up, jnp.logical_and(handler, q < 3))
                go(ref, ref, axz_s.at[near, k, 1], axz_r.at[near, k], down, jnp.logical_and(handler, q > 0))

        agx_own((0, 1, 2))

    ref = block(wh, near, x, zcols)
    go(ref, ref, agx_s.at[near, 0], agx_r.at[near, 0], right, handler)
    go(ref, ref, agx_s.at[near, 1], agx_r.at[near, 1], left, handler)

    local_in[3].wait()

    def normed_rows(source, col, base):
        def run(i, _):
            spot = pl.ds(pl.multiple_of(i * 16, 16), 16)
            there = pl.ds(pl.multiple_of(base + i * 16, 16), 16)
            scale = inv[there, :][:, :1]
            factor = 1.0 + gain_v[:, pl.ds(hcol, H)]
            raw = source[spot, pl.ds(col, H)].astype(F32)
            normed[there, :] = (raw * scale * factor).astype(BF16)
            return 0

        lax.fori_loop(0, T // 16, run, 0)

    normed_rows(res, hcol, 0)

    far_node = jnp.logical_not(handler)
    if NX:
        got(block(wh, own, xo, xcols, 0), axx_r.at[2], handler)
        got(block(wh, own, xo, xcols, 1), axx_r.at[3], handler)
        agx_own((3,))

    ref = block(wh, near, x, zcols)
    target = 2 * c + near
    got(ref, agz_r.at[near], far_node)
    go(ref, ref, agz_s.at[near, 0], agz_r.at[near], up, jnp.logical_and(far_node, jnp.logical_and(q >= target, q < 3)))
    go(ref, ref, agz_s.at[near, 1], agz_r.at[near], down, jnp.logical_and(far_node, jnp.logical_and(q <= target, q > 0)))
    go(ref, ref, agx_s.at[near, 0], agx_r.at[near, 0], right, far_node)
    go(ref, ref, agx_s.at[near, 1], agx_r.at[near, 1], left, far_node)

    got(inv_other, part_r.at[3])
    got(resp, part_r.at[1])
    normed_rows(resp, 0, T)

    local_in[2].wait()
    got(cot.at[pl.ds(T, T)], part_r.at[2])

    def grad_rows(zl):
        def run(t, _):
            at = zl * ZR + t * TILE
            a = normed[:, pl.ds(pl.multiple_of(at, 128), TILE)]
            part = lax.dot_general(a, cot[...], (((0,), (0,)), ((), ())), preferred_element_type=F32)
            g[pl.ds(pl.multiple_of(at, 16), TILE), :] = (part * out_scale).astype(BF16)
            return 0

        lax.fori_loop(0, ZR // TILE, run, 0)

    def add_into(row, count, cols, terms, cond=None):
        step = 48

        def run(i, _):
            spot = pl.ds(pl.multiple_of(row + i * step, 16), step)
            here = pl.ds(pl.multiple_of(i * step, 16), step)
            total = g[spot, cols].astype(F32)
            for term in terms:
                total = total + term[here, :].astype(F32)
            g[spot, cols] = total.astype(BF16)
            return 0

        when(cond, lambda: lax.fori_loop(0, count // step, run, 0))

    def rs_opp(zl):
        go(block(g, zl, xo, zcols, 0), opp.at[zl, 0], rsx_s.at[zl, 0], rsx_r.at[zl, 0], right)
        go(block(g, zl, xo, zcols, 1), opp.at[zl, 1], rsx_s.at[zl, 1], rsx_r.at[zl, 1], left)

    def rs_full(zl):
        got(opp.at[zl, 0], rsx_r.at[zl, 0])
        add_into(rows(zl, xr, 0), R, zcols, [opp.at[zl, 0]])
        go(block(g, zl, xr, zcols), full.at[zl, 0], rsx_s.at[zl, 2], rsx_r.at[zl, 2], right)
        got(opp.at[zl, 1], rsx_r.at[zl, 1])
        add_into(rows(zl, xl, 1), R, zcols, [opp.at[zl, 1]])
        go(block(g, zl, xl, zcols), full.at[zl, 1], rsx_s.at[zl, 3], rsx_r.at[zl, 3], left)

    def rs_z(zl):
        target = 2 * c + zl
        got(full.at[zl, 0], rsx_r.at[zl, 2])
        got(full.at[zl, 1], rsx_r.at[zl, 3])
        add_into(rows(zl, x), SLOT, zcols, [full.at[zl, 0], full.at[zl, 1]])
        above = jnp.logical_and(q >= target, q < 3)
        below = jnp.logical_and(q <= target, q > 0)
        got(zbuf.at[zl, 1], rsz_r.at[zl, 1], above)
        add_into(rows(zl, x), SLOT, zcols, [zbuf.at[zl, 1]], above)
        got(zbuf.at[zl, 0], rsz_r.at[zl, 0], below)
        add_into(rows(zl, x), SLOT, zcols, [zbuf.at[zl, 0]], below)
        ref = block(g, zl, x, zcols)
        go(ref, zbuf.at[zl, 1], rsz_s.at[zl, 0], rsz_r.at[zl, 1], down, q > target)
        go(ref, zbuf.at[zl, 0], rsz_s.at[zl, 1], rsz_r.at[zl, 0], up, q < target)

    def rsx_z(zl, slots=(3, 1, 2, 0)):
        target = 2 * c + zl
        above = jnp.logical_and(q >= target, q < 3)
        below = jnp.logical_and(q <= target, q > 0)
        for k in slots:
            xx = (x, xl, xr, xo)[k]
            got(zxbuf.at[zl, 1, k], rxz_r.at[zl, 1, k], above)
            add_into(rows(zl, xx), SLOT, xcols, [zxbuf.at[zl, 1, k]], above)
            got(zxbuf.at[zl, 0, k], rxz_r.at[zl, 0, k], below)
            add_into(rows(zl, xx), SLOT, xcols, [zxbuf.at[zl, 0, k]], below)
            ref = block(g, zl, xx, xcols)
            go(ref, zxbuf.at[zl, 1, k], rxz_s.at[zl, 0, k], rxz_r.at[zl, 1, k], down, q > target)
            go(ref, zxbuf.at[zl, 0, k], rxz_s.at[zl, 1, k], rxz_r.at[zl, 0, k], up, q < target)

    def outer_start():
        local_in[4].wait()
        local_in[5].wait()
        for b in range(R // (FRAGS * FR_ROWS)):
            first = me * (R // FR_ROWS) + b * FRAGS
            spot = pl.ds(b * FR_ROWS, FR_ROWS)
            term = jnp.zeros((FR_ROWS, DV), F32)
            for k in range(FRAGS):
                taken = (frag[first + k] == 0).astype(F32)
                term = term + taken * anchor_v[pl.ds((b * FRAGS + k) * FR_ROWS, FR_ROWS), :]
            for k in range(HIST):
                taken = (delay[0, b] == k + 1).astype(F32)
                term = term - taken * hist_v[k, spot, :]
            oterm[spot, :] = term
        obuf[y] = oterm[:, pl.ds(pl.multiple_of(y * QUART, 128), QUART)]
        for k in range(1, 4):
            yy = (y + k) % 4
            go(
                oterm.at[:, pl.ds(pl.multiple_of(yy * QUART, 128), QUART)], obuf.at[y],
                oy_s.at[k], oy_r.at[k], {"replica": yy * 2 + zh},
            )

    def outer_mid():
        for k in range(1, 4):
            got(obuf.at[(y + 4 - k) % 4], oy_r.at[k])
        osum[...] = (obuf[0] + obuf[1]) + (obuf[2] + obuf[3])
        go(osum, ozh, oz_s, oz_r, {"replica": y * 2 + 1 - zh})

    def outer_last():
        got(ozh, oz_r)
        mine = pl.ds(pl.multiple_of(y * QUART, 128), QUART)
        od[:, mine] = (osum[...] + ozh[...]) * 0.125
        for k in range(1, 4):
            go(od.at[:, mine], od.at[:, mine], ob_s.at[k], ob_r.at[k], {"replica": ((y + k) % 4) * 2 + zh})

    def outer_out():
        for k in range(1, 4):
            theirs = pl.ds(pl.multiple_of(((y + 4 - k) % 4) * QUART, 128), QUART)
            got(od.at[:, theirs], ob_r.at[k])

    def near_far_values(zl, first):
        def run(n, _):
            cols = pl.ds(pl.multiple_of(n * 256, 128), 256)
            part = jnp.dot(
                normed[:, pl.ds(pl.multiple_of(zl * ZR, 128), ZR)],
                wh[pl.ds(pl.multiple_of(zl * ZR, 16), ZR), cols],
                preferred_element_type=F32,
            )
            if first:
                vacc[:, cols] = part
            else:
                vacc[:, cols] = vacc[:, cols] + part
            return 0

        lax.fori_loop(0, DV // 256, run, 0)

    def dnormed(zl):
        def run(t, _):
            at = zl * ZR + t * TILE
            part = lax.dot_general(
                cot[...], wh[pl.ds(pl.multiple_of(at, 16), TILE), :], (((1,), (1,)), ((), ())),
                preferred_element_type=F32,
            )
            dn[:, pl.ds(pl.multiple_of(at, 128), TILE)] = part * out_scale
            return 0

        lax.fori_loop(0, ZR // TILE, run, 0)

    def sums(zl, first):
        at = pl.multiple_of(zl * ZR, 128)
        factor = 1.0 + gain_v[:, pl.ds(pl.multiple_of(hcol + at, 128), ZR)]

        def part_of(source, col, base, total):
            def run(i, total):
                spot = pl.ds(pl.multiple_of(i * 16, 16), 16)
                there = pl.ds(pl.multiple_of(base + i * 16, 16), 16)
                unit = source[spot, pl.ds(col, ZR)].astype(F32) * inv[there, :][:, :1]
                prod = dn[there, pl.ds(at, ZR)] * unit
                scaled = prod * factor
                lanes = scaled[:, :128]
                for k in range(1, ZR // 128):
                    lanes = lanes + scaled[:, k * 128 : (k + 1) * 128]
                if first:
                    rs[there, :] = lanes
                else:
                    rs[there, :] = rs[there, :] + lanes
                return total + (prod[:8] + prod[8:])

            return lax.fori_loop(0, T // 16, run, total)

        total = jnp.zeros((8, ZR), F32)
        total = part_of(res, pl.multiple_of(hcol + at, 128), 0, total)
        total = part_of(resp, at, T, total)
        ggt[:, pl.ds(at, ZR)] = jnp.sum(total, axis=0, keepdims=True)

    def input_grad(source, col, base):
        factor = 1.0 + gain_v[:, pl.ds(hcol, H)]

        def run(i, _):
            spot = pl.ds(pl.multiple_of(i * 16, 16), 16)
            there = pl.ds(pl.multiple_of(base + i * 16, 16), 16)
            scale = inv[there, :][:, :1]
            unit = source[spot, pl.ds(col, H)].astype(F32) * scale
            there_too = pl.ds(pl.multiple_of(T - base + i * 16, 16), 16)
            mean = jnp.sum(rs[there, :] + rsp[there_too, :], axis=1, keepdims=True) * (1.0 / D)
            ig[there, :] = (scale * (dn[there, :] * factor - unit * mean)).astype(BF16)
            return 0

        lax.fori_loop(0, T // 16, run, 0)

    grad_rows(far)
    rs_opp(far)
    ag_fwd(near)
    grad_rows(near)
    rs_opp(near)
    if NX:
        rsx_z(far)
    rs_full(far)
    outer_start()
    if NX:
        target = 2 * c + near
        for k in range(4):
            xx = (x, xl, xr, xo)[k]
            ref = block(wh, near, xx, xcols)
            got(ref, axz_r.at[near, k], far_node)
            go(ref, ref, axz_s.at[near, k, 0], axz_r.at[near, k], up,
               jnp.logical_and(far_node, jnp.logical_and(q >= target, q < 3)))
            go(ref, ref, axz_s.at[near, k, 1], axz_r.at[near, k], down,
               jnp.logical_and(far_node, jnp.logical_and(q <= target, q > 0)))
    ag_z(far)
    ag_x(far)
    rs_full(near)
    if NX:
        rsx_z(near)
    outer_mid()
    ag_fwd(far)
    rs_z(far)
    if NX:
        agx_zsend(far, range(4))
    outer_last()
    ag_end(near)
    near_far_values(near, True)
    dnormed(near)
    rs_z(near)

    def rs_last():
        if NX:
            go(block(g, own, xo, xcols, 0), oppx.at[0], rxx_s.at[0], rxx_r.at[0], right, handler)
            go(block(g, own, xo, xcols, 1), oppx.at[1], rxx_s.at[1], rxx_r.at[1], left, handler)

    rs_last()
    sums(near, True)
    if NX:
        got(oppx.at[0], rxx_r.at[0], handler)
        add_into(rows(own, xr, 0), R, xcols, [oppx.at[0]], handler)
        go(block(g, own, xr, xcols), fullx.at[0], rxx_s.at[2], rxx_r.at[2], right, handler)
        got(oppx.at[1], rxx_r.at[1], handler)
        add_into(rows(own, xl, 1), R, xcols, [oppx.at[1]], handler)
        go(block(g, own, xl, xcols), fullx.at[1], rxx_s.at[3], rxx_r.at[3], left, handler)
    outer_out()
    delta_out = pltpu.make_async_copy(od, delta_o, loc.at[6])
    delta_out.start()

    ag_end(far)
    near_far_values(far, False)
    other_tokens = pl.ds(T, T)
    go(vacc.at[other_tokens], vrecv, part_s.at[4], part_r.at[4], partner)
    dnormed(far)
    sums(far, False)
    go(rs, rsp, part_s.at[5], part_r.at[5], partner)
    ggx[x] = ggt[...]
    for k in range(1, 4):
        go(ggx.at[x], ggx.at[x], gx_s.at[k], gx_r.at[k], dev(q, (x + k) % 4, c))
    got(rsp, part_r.at[5])
    input_grad(resp, 0, T)
    go(ig.at[other_tokens], igrad_o.at[0, :, pl.ds(hcol, H)], part_s.at[6], part_r.at[6], partner)
    for k in range(1, 4):
        got(ggx.at[(x + 4 - k) % 4], gx_r.at[k])
    ggz[q] = (ggx[0] + ggx[1]) + (ggx[2] + ggx[3])
    for k in range(1, 4):
        go(ggz.at[q], ggz.at[q], gz_s.at[k], gz_r.at[k], dev((q + k) % 4, x, c))
    input_grad(res, hcol, 0)
    ig_out = pltpu.make_async_copy(ig.at[pl.ds(0, T)], igrad_o.at[0, :, pl.ds(hcol, H)], loc.at[7])
    ig_out.start()
    got(vrecv, part_r.at[4])
    vout[...] = ((vacc[pl.ds(0, T), :] + vrecv[...]) * out_scale).astype(BF16)
    values_out = pltpu.make_async_copy(vout, values_o.at[0], loc.at[8])
    values_out.start()
    for k in range(1, 4):
        got(ggz.at[(q + 4 - k) % 4], gz_r.at[k])
    ggt[...] = (ggz[0] + ggz[1]) + (ggz[2] + ggz[3])
    gg_out = pltpu.make_async_copy(ggt, ggrad_o.at[:, pl.ds(hcol, H)], loc.at[9])
    gg_out.start()
    go(ggt, ggrad_o.at[:, pl.ds(hcol, H)], part_s.at[7], part_r.at[7], partner)

    if NX:
        got(fullx.at[0], rxx_r.at[2], handler)
        got(fullx.at[1], rxx_r.at[3], handler)
        add_into(rows(own, x), SLOT, xcols, [fullx.at[0], fullx.at[1]], handler)

    grad_mine = pltpu.make_async_copy(g.at[own_rows, :], grad_o, loc.at[10])
    when(handler, lambda: grad_mine.start())
    go(g.at[other_rows, :], grad_o, part_s.at[8], part_r.at[8], partner, handler)
    got(grad_o, part_r.at[8], far_node)
    got(igrad_o.at[0, :, pl.ds(pcol, H)], part_r.at[6])
    got(ggrad_o.at[:, pl.ds(pcol, H)], part_r.at[7])

    when(handler, lambda: grad_mine.wait())
    for item in (delta_out, ig_out, values_out, gg_out):
        item.wait()
    for cond, made in sends:
        when(cond, lambda made=made: made.wait_send())


def main_call(frag, delay, residual, cotangent, gain, master, anchor, history):
    any_space = pl.BlockSpec(memory_space=pl.ANY)
    smem = pl.BlockSpec(memory_space=pltpu.SMEM)
    vm = pltpu.VMEM
    dma = pltpu.SemaphoreType.DMA
    nx = max(NX, 128)
    scratch = [
        vm((T, D), BF16), vm((T, H), BF16), vm((2 * T, DV), BF16), vm((1, D), F32),
        vm((R, DV), F32), vm((R, DV), F32), vm((HIST, PART, DV), F32),
        vm((H, DV), BF16), vm((R, DV), BF16), vm((H, DV), BF16), vm((2 * T, H), BF16),
        vm((2 * T, 128), F32), vm((2 * T, H), F32), vm((2 * T, DV), F32), vm((T, DV), F32),
        vm((T, DV), BF16), vm((2 * T, 128), F32), vm((2 * T, 128), F32), vm((2 * T, H), BF16),
        vm((4, 1, H), F32), vm((4, 1, H), F32), vm((1, H), F32),
        vm((2, 2, R, NZ), BF16), vm((2, 2, SLOT, NZ), BF16), vm((2, 2, SLOT, NZ), BF16),
        vm((2, 2, 4, SLOT, nx), BF16), vm((2, R, nx), BF16), vm((2, SLOT, nx), BF16),
        vm((PART, DV), F32), vm((4, PART, QUART), F32), vm((PART, QUART), F32),
        vm((PART, QUART), F32), vm((PART, DV), F32),
        dma((11,)), dma((9,)), dma((9,)), dma((2, 2)), dma((2,)), dma((2, 4)), dma((2, 4)),
        dma((4,)), dma((4,)), dma((2, 4, 2)), dma((2, 4)),
        dma((2, 4)), dma((2, 4)), dma((2, 2)), dma((2, 2)),
        dma((2, 2, 4)), dma((2, 2, 4)), dma((4,)), dma((4,)),
        dma((4,)), dma((4,)), dma((4,)), dma((4,)),
        dma((4,)), dma((4,)), dma, dma, dma((4,)), dma((4,)),
    ]
    return pl.pallas_call(
        main_kernel,
        out_shape=(
            jax.ShapeDtypeStruct((1, T, DV), BF16),
            jax.ShapeDtypeStruct((1, T, D), BF16),
            jax.ShapeDtypeStruct((1, D), F32),
            jax.ShapeDtypeStruct((R, DV), BF16),
            jax.ShapeDtypeStruct((PART, DV), F32),
        ),
        in_specs=[smem, smem] + [any_space] * 6,
        out_specs=(any_space,) * 5,
        scratch_shapes=scratch,
        compiler_params=pltpu.CompilerParams(
            collective_id=0, has_side_effects=True, vmem_limit_bytes=52 * 1024 * 1024
        ),
        name="inner_step",
    )(frag, delay, residual, cotangent, gain, master, anchor, history)


def update_kernel(frag, grad, master, first, second, anchor, momentum, delta,
                  master_o, first_o, second_o, anchor_o, momentum_o):
    group = pl.program_id(0)
    start = lax.axis_index("fsdp") * (R // FR_ROWS) + group * FRAGS
    chosen = jnp.int32(0)
    for k in range(1, FRAGS):
        chosen = chosen + jnp.where(frag[start + k] == 0, k, 0)
    at = pl.ds(pl.multiple_of(chosen * FR_ROWS, FR_ROWS), FR_ROWS)

    gradient = grad[...].astype(F32)
    weights = master[0]
    first_new = beta_one * first[0] + (1.0 - beta_one) * gradient
    second_new = beta_two * second[0] + (1.0 - beta_two) * gradient * gradient
    first_o[0] = first_new
    second_o[0] = second_new
    master_o[0] = weights - inner_rate * (
        first_new / (jnp.sqrt(second_new) + adam_eps) + weight_decay * weights
    )

    change = delta[...]
    anchor_old = anchor[at, :]
    momentum_part = outer_beta * momentum[at, :] + change
    anchor_part = anchor_old - outer_rate * (change + outer_beta * momentum_part)
    anchor_o[...] = anchor[...]
    momentum_o[...] = momentum[...]
    anchor_o[at, :] = anchor_part
    momentum_o[at, :] = momentum_part
    master_o[0, at, :] = mix_weight * master_o[0, at, :] + (1.0 - mix_weight) * anchor_part


def update_call(frag, grad, master, first, second, anchor, momentum, delta):
    rows = FRAGS * FR_ROWS
    flat = pl.BlockSpec((rows, DV), lambda i: (i, 0))
    deep = pl.BlockSpec((1, rows, DV), lambda i: (0, i, 0))
    like3 = jax.ShapeDtypeStruct((1, R, DV), F32)
    like2 = jax.ShapeDtypeStruct((R, DV), F32)
    return pl.pallas_call(
        update_kernel,
        grid=(R // rows,),
        out_shape=(like3, like3, like3, like2, like2),
        in_specs=[
            pl.BlockSpec(memory_space=pltpu.SMEM), flat, deep, deep, deep, flat, flat,
            pl.BlockSpec((FR_ROWS, DV), lambda i: (i, 0)),
        ],
        out_specs=(deep, deep, deep, flat, flat),
        name="update",
    )(frag, grad, master, first, second, anchor, momentum, delta)


def body(
    residual, cotangent, norm_gain, master, first_moment, second_moment,
    anchor, outer_momentum, history, fragment, delay,
):
    values, input_grad, gain_grad, gradient, delta = main_call(
        fragment, delay, residual, cotangent, norm_gain, master, anchor, history
    )
    new_master, new_first, new_second, new_anchor, new_momentum = update_call(
        fragment, gradient, master, first_moment, second_moment, anchor, outer_momentum, delta
    )
    return (
        values, input_grad, gain_grad, new_master, new_first, new_second, new_anchor, new_momentum,
    )


def solution(mesh):
    rows = P("replica", "fsdp", None)
    both = P("fsdp", None)
    return jax.shard_map(
        body,
        mesh=mesh,
        in_specs=(
            rows, rows, P("replica", None), rows, rows, rows, both, both,
            P("replica", None, "fsdp", None), P(), P("replica", "fsdp"),
        ),
        out_specs=(rows, rows, P("replica", None), rows, rows, rows, both, both),
        check_vma=False,
    )
```

time: 265 us -> 170 us (0.64)
  the two profiles are of different devices: /device:TPU:16 before, /device:TPU:1 now
where the time goes in v1:
time: 170 us
  Pallas kernels  161 us (95%)
  local copies, waits for them, and re-layouts  8.25 us (5%)
    pallas_call x1, Pallas kernels, main_call(): pl.pallas_call(main_kernel, out_shape=(jax.ShapeDtypeStruct((1, T, DV), B...  157 us
    unnamed x19, local copies, waits for them, and re-layouts  8.25 us
    pallas_call x1, Pallas kernels, update_call(): pl.pallas_call(update_kernel, grid=(R // rows,), out_shape=(like3, like3,...  4.49 us

profile of v1, /device:TPU:1, one launch (start us, length us, event | category | flops | bytes accessed | tf_op | source)
XLA Modules:
  0.0 170.0 jit_solution(17566674699926256912)
XLA Ops:
  0.6 0.0 copy-start
  0.6 1.0 copy-done
  1.7 0.0 copy-start.1
  1.7 1.0 copy-done.1
  2.7 0.0 copy-start.4
  2.7 0.7 copy-done.4
  3.4 0.0 copy-start.5
  3.4 0.7 copy-done.5
  4.1 0.0 copy-start.6
  4.1 0.7 copy-done.6
  4.7 156.6 %inner_step.1 = (bf16[1,256,1024]{2,1,0:T(8,128)(2,1)S(1)}, bf16[1,256,4608]{2,1,0:T(8,128)(2,1)}, f32[1,4608]{1,0:T(1,128)S(1)}, bf16[144,1024]{1,0:T(8,128)(2,1)S(1)}, f32[24,1024]{1,0:T(8,128)S(1)}) custom-call(s32[576]{0:T(1024)S(1)} %copy-done.5, s32[1,3]{1,0:T(1,128)S(1)} %copy-done.6, bf16[1,256,4608]{2,1,0:T(8,128)(2,1)} %residual.1, ...), custom_call_target="tpu_custom_call" | custom-call | tf_op jit(solution)/shard_map/inner_step/pallas_call | solution.py:560
  161.3 0.0 copy-start.2
  161.3 0.7 copy-done.2
  162.0 0.0 copy-start.3
  162.0 0.6 copy-done.3
  162.7 0.0 copy-start.7
  162.7 4.5 %update.1 = (f32[1,144,1024]{2,1,0:T(8,128)}, f32[1,144,1024]{2,1,0:T(8,128)}, f32[1,144,1024]{2,1,0:T(8,128)}, f32[144,1024]{1,0:T(8,128)}, f32[144,1024]{1,0:T(8,128)}) custom-call(s32[576]{0:T(1024)} %frag.3, bf16[144,1024]{1,0:T(8,128)(2,1)} %copy-done.2, f32[1,144,1024]{2,1,0:T(8,128)} %master.3, f32[1,144,1024]{2,1,0:T(8,128)} %first.1, ...), custom_call_target="tpu_custom_call" | custom-call | tf_op jit(solution)/shard_map/update/pallas_call | solution.py:615
  167.2 0.8 copy.22
  168.0 0.0 copy-done.7
  168.0 1.4 copy.23
  169.4 0.6 copy.24
Async XLA Ops:
  0.6 1.0 copy-start
  1.7 1.0 copy-start.1
  2.7 0.7 copy-start.4
  3.4 0.7 copy-start.5
  4.1 0.7 copy-start.6
  161.3 0.7 copy-start.2
  162.0 0.6 copy-start.3
  162.7 5.3 %copy-start.7 = (bf16[1,256,4608]{2,1,0:T(8,128)(2,1)S(1)}, bf16[1,256,4608]{2,1,0:T(8,128)(2,1)}, u32[]{:S(2)}) copy-start(bf16[1,256,4608]{2,1,0:T(8,128)(2,1)} %get-tuple-element.37) | copy-start | bytes 7077892

commit v2 on v0

v2 whole, which is shorter than its diff:
```python
import jax
import jax.numpy as jnp
from jax import lax
from jax.experimental import pallas as pl
from jax.experimental.pallas import tpu as pltpu
from jax.sharding import PartitionSpec as P

D = 4608
DV = 1024
FRAGS = 6
FR_ROWS = 8
HIST = 4

T = 256
R = 144
SLOT = 2 * R
ZR = 4 * SLOT
H = 2 * ZR
TILE = 384
NZ = 640
NX = DV - NZ
PART = R // FRAGS
QUART = DV // 4

norm_eps = 1e-06
beta_one = 0.9
beta_two = 0.95
inner_rate = 0.01
weight_decay = 0.1
adam_eps = 1e-08
outer_beta = 0.9
outer_rate = 0.7
mix_weight = 0.5
out_scale = float(D) ** (-0.5)

MESH = pl.DeviceIdType.MESH
F32 = jnp.float32
BF16 = jnp.bfloat16


ORDERS = [
    [
        0, 1, 3, 11, 7, 2, 5, 4, 8, 51, 31, 6, 32, 10, 9, 53, 13, 33, 19, 12, 65, 52, 66, 67, 20, 64, 54, 40,
        34, 55, 56, 68, 70, 61, 41, 71, 69, 21, 35, 42, 63, 57, 58, 24, 36, 48, 37, 22, 62, 47, 49, 59, 27,
        50, 14, 60, 23, 15, 16, 25, 29, 26, 38, 28, 39, 17, 18,
    ],
    [
        0, 1, 3, 11, 2, 7, 4, 8, 5, 12, 51, 32, 64, 6, 13, 31, 65, 10, 19, 9, 20, 67, 33, 66, 34, 53, 52, 55,
        40, 41, 56, 54, 42, 61, 69, 57, 68, 58, 21, 35, 47, 62, 70, 63, 71, 50, 59, 24, 49, 48, 14, 37, 23,
        36, 25, 60, 15, 16, 27, 26, 38, 22, 17, 29, 39, 18, 28,
    ],
    [
        11, 13, 12, 30, 43, 55, 34, 51, 65, 56, 19, 35, 45, 32, 71, 52, 68, 69, 70, 31, 53, 58, 46, 64, 20,
        57, 44, 67, 37, 66, 47, 50, 36, 33, 49, 54, 48, 21, 40, 42, 59, 61, 63, 38, 60, 41, 24, 62, 39, 23,
        25, 27, 22, 26, 28, 29,
    ],
    [
        11, 19, 13, 12, 55, 68, 56, 69, 34, 71, 70, 58, 35, 48, 50, 57, 49, 47, 30, 43, 51, 20, 32, 45, 31,
        36, 59, 60, 37, 44, 46, 53, 21, 65, 52, 33, 64, 40, 41, 38, 42, 22, 67, 39, 66, 54, 61, 63, 24, 62,
        23, 25, 27, 29, 28, 26,
    ],
]


def step(number, run):
    run()


def main_kernel(
    frag, delay, residual, cotangent, gain, master, anchor, history,
    values_o, igrad_o, ggrad_o, grad_o, delta_o,
    res, resp, cot, gain_v, master_v, anchor_v, hist_v,
    wh, stage, g, normed, inv, dn, vacc, vrecv, vout, rs, rsp, ig, ggx, ggz, ggt,
    opp, full, zbuf, zxbuf, oppx, fullx, oterm, obuf, osum, ozh, od,
    loc, part_s, part_r, agz_s, agz_r, agx_s, agx_r, axx_s, axx_r, axz_s, axz_r,
    rsx_s, rsx_r, rsz_s, rsz_r, rxz_s, rxz_r, rxx_s, rxx_r, gx_s, gx_r, gz_s, gz_r,
    oy_s, oy_r, oz_s, oz_r, ob_s, ob_r,
):
    me = lax.axis_index("fsdp")
    rep = lax.axis_index("replica")
    q, x, c = me // 8, (me // 2) % 4, me % 2
    y, zh = rep // 2, rep % 2
    xr, xl, xo = (x + 1) % 4, (x + 3) % 4, (x + 2) % 4
    handler = c == q // 2
    place = jnp.where(c == 0, q, 3 - q)
    near = jnp.where(place == 0, c, 1 - c)
    far = 1 - near

    def dev(qq, xx, cc):
        return {"fsdp": qq * 8 + xx * 2 + cc}

    partner, right, left = dev(q, x, 1 - c), dev(q, xr, c), dev(q, xl, c)
    up, down = dev(q + 1, x, c), dev(q - 1, x, c)

    sends = []

    def copy(src, dst, send, recv, to):
        return pltpu.make_async_remote_copy(
            src_ref=src, dst_ref=dst, send_sem=send, recv_sem=recv, device_id=to, device_id_type=MESH
        )

    def when(cond, run):
        if cond is True:
            run()
        elif cond is not False:
            @pl.when(cond)
            def _():
                run()

    def go(src, dst, send, recv, to, cond=True):
        made = copy(src, dst, send, recv, to)
        when(cond, lambda: made.start())
        sends.append((cond, made))

    def got(dst, recv, cond=True):
        made = copy(dst, dst, part_s.at[0], recv, partner)
        when(cond, lambda: made.wait_recv())

    local_in = [
        pltpu.make_async_copy(master.at[0], master_v, loc.at[0]),
        pltpu.make_async_copy(residual.at[0], res, loc.at[1]),
        pltpu.make_async_copy(cotangent.at[0], cot.at[pl.ds(0, T)], loc.at[2]),
        pltpu.make_async_copy(gain, gain_v, loc.at[3]),
        pltpu.make_async_copy(anchor, anchor_v, loc.at[4]),
        pltpu.make_async_copy(history.at[0], hist_v, loc.at[5]),
    ]
    for item in local_in:
        item.start()

    barrier = pltpu.get_barrier_semaphore()
    greeted = [partner]
    greeted += [dev(q, (x + k) % 4, c) for k in range(1, 4)]
    greeted += [dev((q + k) % 4, x, c) for k in range(1, 4)]
    greeted += [{"replica": ((y + k) % 4) * 2 + zh} for k in range(1, 4)]
    greeted += [{"replica": y * 2 + 1 - zh}]
    for to in greeted:
        pl.semaphore_signal(barrier, inc=1, device_id=to, device_id_type=MESH)
    pl.semaphore_wait(barrier, len(greeted))

    zcols, xcols = pl.ds(0, NZ), pl.ds(NZ, NX)

    def rows(zl, xx, half=0):
        return pl.multiple_of(zl * ZR + xx * SLOT + half * R, 16)

    def block(buf, zl, xx, cols, half=None):
        if half is None:
            return buf.at[pl.ds(rows(zl, xx), SLOT), cols]
        return buf.at[pl.ds(rows(zl, xx, half), R), cols]

    hcol = pl.multiple_of(c * H, 128)
    pcol = pl.multiple_of((1 - c) * H, 128)

    own = q % 2
    local_in[0].wait()
    own_rows = pl.ds(pl.multiple_of(own * ZR + x * SLOT + c * R, 16), R)

    @pl.when(handler)
    def _():
        wh[own_rows, :] = master_v[...].astype(BF16)

    @pl.when(jnp.logical_not(handler))
    def _():
        stage[...] = master_v[...].astype(BF16)

    go(stage, wh.at[own_rows, :], part_s.at[0], part_r.at[0], partner, jnp.logical_not(handler))
    other_rows = pl.ds(pl.multiple_of(own * ZR + x * SLOT + (1 - c) * R, 16), R)

    go(residual.at[0, :, pl.ds(pcol, H)], resp, part_s.at[1], part_r.at[1], partner)
    go(cotangent.at[0], cot.at[pl.ds(T, T)], part_s.at[2], part_r.at[2], partner)

    first_sends = len(sends)

    def all_steps(owner, order):
        def slot_of(k):
            return (x, xl, xr, xo)[k]

        def towards(zl):
            goal = 2 * c + zl
            return jnp.logical_and(q >= goal, q < 3), jnp.logical_and(q <= goal, q > 0)

        def both(fixed, cond):
            return cond if fixed else False

        def own_in():
            got(wh.at[other_rows, :], part_r.at[0], owner)

        def ag_z_send(zl, cond):
            ref = block(wh, zl, x, zcols)
            go_up, go_down = towards(zl)
            go(ref, ref, agz_s.at[zl, 0], agz_r.at[zl], up, both(cond, go_up))
            go(ref, ref, agz_s.at[zl, 1], agz_r.at[zl], down, both(cond, go_down))

        def ag_x_send(zl, cond):
            ref = block(wh, zl, x, zcols)
            go(ref, ref, agx_s.at[zl, 0], agx_r.at[zl, 0], right, cond)
            go(ref, ref, agx_s.at[zl, 1], agx_r.at[zl, 1], left, cond)

        def ag_z(zl):
            cond = not (owner and zl is near)
            got(block(wh, zl, x, zcols), agz_r.at[zl], cond)
            ag_z_send(zl, cond)
            ag_x_send(zl, cond)

        def ag_left(zl):
            got(block(wh, zl, xl, zcols), agx_r.at[zl, 0])
            ref = block(wh, zl, xl, zcols, 0)
            go(ref, ref, agx_s.at[zl, 2], agx_r.at[zl, 2], right)

        def ag_right(zl):
            got(block(wh, zl, xr, zcols), agx_r.at[zl, 1])
            ref = block(wh, zl, xr, zcols, 1)
            go(ref, ref, agx_s.at[zl, 3], agx_r.at[zl, 3], left)

        def ag_end(zl):
            got(block(wh, zl, xo, zcols, 0), agx_r.at[zl, 2])
            got(block(wh, zl, xo, zcols, 1), agx_r.at[zl, 3])

        def ax_send():
            ref = block(wh, own, x, xcols)
            go(ref, ref, axx_s.at[0], axx_r.at[0], right, owner)
            go(ref, ref, axx_s.at[1], axx_r.at[1], left, owner)

        def ax_left():
            got(block(wh, own, xl, xcols), axx_r.at[0], owner)
            ref = block(wh, own, xl, xcols, 0)
            go(ref, ref, axx_s.at[2], axx_r.at[2], right, owner)

        def ax_right():
            got(block(wh, own, xr, xcols), axx_r.at[1], owner)
            ref = block(wh, own, xr, xcols, 1)
            go(ref, ref, axx_s.at[3], axx_r.at[3], left, owner)

        def ax_end():
            got(block(wh, own, xo, xcols, 0), axx_r.at[2], owner)
            got(block(wh, own, xo, xcols, 1), axx_r.at[3], owner)

        def ax_z_send(zl, k, cond):
            ref = block(wh, zl, slot_of(k), xcols)
            go_up, go_down = towards(zl)
            go(ref, ref, axz_s.at[zl, k, 0], axz_r.at[zl, k], up, both(cond, go_up))
            go(ref, ref, axz_s.at[zl, k, 1], axz_r.at[zl, k], down, both(cond, go_down))

        def ax_own(k):
            ax_z_send(near, k, owner)

        def ax_z(zl, k):
            cond = not (owner and zl is near)
            got(block(wh, zl, slot_of(k), xcols), axz_r.at[zl, k], cond)
            ax_z_send(zl, k, cond)

        def norm_rows(i, _):
            spot = pl.ds(pl.multiple_of(i * 16, 16), 16)
            raw = res[spot, :].astype(F32)
            scale = lax.rsqrt(jnp.mean(raw * raw, axis=1, keepdims=True) + norm_eps)
            inv[spot, :] = jnp.broadcast_to(scale, (16, 128))
            return 0

        def scales():
            local_in[3].wait()
            local_in[1].wait()
            lax.fori_loop(0, T // 16, norm_rows, 0)
            go(inv.at[pl.ds(0, T)], inv.at[pl.ds(T, T)], part_s.at[3], part_r.at[3], partner)

        def normed_rows(source, col, base):
            def run(i, _):
                spot = pl.ds(pl.multiple_of(i * 16, 16), 16)
                there = pl.ds(pl.multiple_of(base + i * 16, 16), 16)
                scale = inv[there, :][:, :1]
                factor = 1.0 + gain_v[:, pl.ds(hcol, H)]
                raw = source[spot, pl.ds(col, H)].astype(F32)
                normed[there, :] = (raw * scale * factor).astype(BF16)
                return 0

            lax.fori_loop(0, T // 16, run, 0)

        def normed_own():
            normed_rows(res, hcol, 0)

        def normed_other():
            got(inv.at[pl.ds(T, T)], part_r.at[3])
            got(resp, part_r.at[1])
            normed_rows(resp, 0, T)
            local_in[2].wait()
            got(cot.at[pl.ds(T, T)], part_r.at[2])

        def grad_rows(zl):
            def run(t, _):
                at = zl * ZR + t * TILE
                a = normed[:, pl.ds(pl.multiple_of(at, 128), TILE)]
                part = lax.dot_general(a, cot[...], (((0,), (0,)), ((), ())), preferred_element_type=F32)
                g[pl.ds(pl.multiple_of(at, 16), TILE), :] = (part * out_scale).astype(BF16)
                return 0

            lax.fori_loop(0, ZR // TILE, run, 0)

        def add_into(row, count, cols, terms, cond=True):
            step = 48

            def run(i, _):
                spot = pl.ds(pl.multiple_of(row + i * step, 16), step)
                here = pl.ds(pl.multiple_of(i * step, 16), step)
                total = g[spot, cols].astype(F32)
                for term in terms:
                    total = total + term[here, :].astype(F32)
                g[spot, cols] = total.astype(BF16)
                return 0

            when(cond, lambda: lax.fori_loop(0, count // step, run, 0))

        def rs_opp(zl):
            go(block(g, zl, xo, zcols, 0), opp.at[zl, 0], rsx_s.at[zl, 0], rsx_r.at[zl, 0], right)
            go(block(g, zl, xo, zcols, 1), opp.at[zl, 1], rsx_s.at[zl, 1], rsx_r.at[zl, 1], left)

        def rs_right(zl):
            got(opp.at[zl, 0], rsx_r.at[zl, 0])
            add_into(rows(zl, xr, 0), R, zcols, [opp.at[zl, 0]])
            go(block(g, zl, xr, zcols), full.at[zl, 0], rsx_s.at[zl, 2], rsx_r.at[zl, 2], right)

        def rs_left(zl):
            got(opp.at[zl, 1], rsx_r.at[zl, 1])
            add_into(rows(zl, xl, 1), R, zcols, [opp.at[zl, 1]])
            go(block(g, zl, xl, zcols), full.at[zl, 1], rsx_s.at[zl, 3], rsx_r.at[zl, 3], left)

        def rs_x(zl):
            got(full.at[zl, 0], rsx_r.at[zl, 2])
            got(full.at[zl, 1], rsx_r.at[zl, 3])
            add_into(rows(zl, x), SLOT, zcols, [full.at[zl, 0], full.at[zl, 1]])

        def rs_z(zl):
            above, below = towards(zl)
            got(zbuf.at[zl, 1], rsz_r.at[zl, 1], above)
            add_into(rows(zl, x), SLOT, zcols, [zbuf.at[zl, 1]], above)
            got(zbuf.at[zl, 0], rsz_r.at[zl, 0], below)
            add_into(rows(zl, x), SLOT, zcols, [zbuf.at[zl, 0]], below)
            ref = block(g, zl, x, zcols)
            goal = 2 * c + zl
            go(ref, zbuf.at[zl, 1], rsz_s.at[zl, 0], rsz_r.at[zl, 1], down, q > goal)
            go(ref, zbuf.at[zl, 0], rsz_s.at[zl, 1], rsz_r.at[zl, 0], up, q < goal)

        def rx_z(zl, k):
            above, below = towards(zl)
            xx = slot_of(k)
            got(zxbuf.at[zl, 1, k], rxz_r.at[zl, 1, k], above)
            add_into(rows(zl, xx), SLOT, xcols, [zxbuf.at[zl, 1, k]], above)
            got(zxbuf.at[zl, 0, k], rxz_r.at[zl, 0, k], below)
            add_into(rows(zl, xx), SLOT, xcols, [zxbuf.at[zl, 0, k]], below)
            ref = block(g, zl, xx, xcols)
            goal = 2 * c + zl
            go(ref, zxbuf.at[zl, 1, k], rxz_s.at[zl, 0, k], rxz_r.at[zl, 1, k], down, q > goal)
            go(ref, zxbuf.at[zl, 0, k], rxz_s.at[zl, 1, k], rxz_r.at[zl, 0, k], up, q < goal)

        def rx_opp():
            go(block(g, own, xo, xcols, 0), oppx.at[0], rxx_s.at[0], rxx_r.at[0], right, owner)
            go(block(g, own, xo, xcols, 1), oppx.at[1], rxx_s.at[1], rxx_r.at[1], left, owner)

        def rx_right():
            got(oppx.at[0], rxx_r.at[0], owner)
            add_into(rows(own, xr, 0), R, xcols, [oppx.at[0]], owner)
            go(block(g, own, xr, xcols), fullx.at[0], rxx_s.at[2], rxx_r.at[2], right, owner)

        def rx_left():
            got(oppx.at[1], rxx_r.at[1], owner)
            add_into(rows(own, xl, 1), R, xcols, [oppx.at[1]], owner)
            go(block(g, own, xl, xcols), fullx.at[1], rxx_s.at[3], rxx_r.at[3], left, owner)

        def rx_end():
            got(fullx.at[0], rxx_r.at[2], owner)
            got(fullx.at[1], rxx_r.at[3], owner)
            add_into(rows(own, x), SLOT, xcols, [fullx.at[0], fullx.at[1]], owner)

        grad_mine = pltpu.make_async_copy(g.at[own_rows, :], grad_o, loc.at[10])

        def grad_out():
            when(owner, lambda: grad_mine.start())
            go(g.at[other_rows, :], grad_o, part_s.at[8], part_r.at[8], partner, owner)

        def outer_start():
            local_in[4].wait()
            local_in[5].wait()
            for b in range(R // (FRAGS * FR_ROWS)):
                first = me * (R // FR_ROWS) + b * FRAGS
                spot = pl.ds(b * FR_ROWS, FR_ROWS)
                term = jnp.zeros((FR_ROWS, DV), F32)
                for k in range(FRAGS):
                    taken = (frag[first + k] == 0).astype(F32)
                    term = term + taken * anchor_v[pl.ds((b * FRAGS + k) * FR_ROWS, FR_ROWS), :]
                for k in range(HIST):
                    taken = (delay[0, b] == k + 1).astype(F32)
                    term = term - taken * hist_v[k, spot, :]
                oterm[spot, :] = term
            obuf[y] = oterm[:, pl.ds(pl.multiple_of(y * QUART, 128), QUART)]
            for k in range(1, 4):
                yy = (y + k) % 4
                go(
                    oterm.at[:, pl.ds(pl.multiple_of(yy * QUART, 128), QUART)], obuf.at[y],
                    oy_s.at[k], oy_r.at[k], {"replica": yy * 2 + zh},
                )

        def outer_mid():
            for k in range(1, 4):
                got(obuf.at[(y + 4 - k) % 4], oy_r.at[k])
            osum[...] = (obuf[0] + obuf[1]) + (obuf[2] + obuf[3])
            go(osum, ozh, oz_s, oz_r, {"replica": y * 2 + 1 - zh})

        def outer_last():
            got(ozh, oz_r)
            mine = pl.ds(pl.multiple_of(y * QUART, 128), QUART)
            od[:, mine] = (osum[...] + ozh[...]) * 0.125
            for k in range(1, 4):
                go(od.at[:, mine], od.at[:, mine], ob_s.at[k], ob_r.at[k], {"replica": ((y + k) % 4) * 2 + zh})

        def outer_out():
            for k in range(1, 4):
                theirs = pl.ds(pl.multiple_of(((y + 4 - k) % 4) * QUART, 128), QUART)
                got(od.at[:, theirs], ob_r.at[k])

        def near_far_values(zl, first):
            def run(n, _):
                cols = pl.ds(pl.multiple_of(n * 256, 128), 256)
                part = jnp.dot(
                    normed[:, pl.ds(pl.multiple_of(zl * ZR, 128), ZR)],
                    wh[pl.ds(pl.multiple_of(zl * ZR, 16), ZR), cols],
                    preferred_element_type=F32,
                )
                if first:
                    vacc[:, cols] = part
                else:
                    vacc[:, cols] = vacc[:, cols] + part
                return 0

            lax.fori_loop(0, DV // 256, run, 0)

        def dnormed(zl):
            def run(t, _):
                at = zl * ZR + t * TILE
                part = lax.dot_general(
                    cot[...], wh[pl.ds(pl.multiple_of(at, 16), TILE), :], (((1,), (1,)), ((), ())),
                    preferred_element_type=F32,
                )
                dn[:, pl.ds(pl.multiple_of(at, 128), TILE)] = part * out_scale
                return 0

            lax.fori_loop(0, ZR // TILE, run, 0)

        def sums(zl, first):
            at = pl.multiple_of(zl * ZR, 128)
            factor = 1.0 + gain_v[:, pl.ds(pl.multiple_of(hcol + at, 128), ZR)]

            def part_of(source, col, base, total):
                def run(i, total):
                    spot = pl.ds(pl.multiple_of(i * 16, 16), 16)
                    there = pl.ds(pl.multiple_of(base + i * 16, 16), 16)
                    unit = source[spot, pl.ds(col, ZR)].astype(F32) * inv[there, :][:, :1]
                    prod = dn[there, pl.ds(at, ZR)] * unit
                    scaled = prod * factor
                    lanes = scaled[:, :128]
                    for k in range(1, ZR // 128):
                        lanes = lanes + scaled[:, k * 128 : (k + 1) * 128]
                    if first:
                        rs[there, :] = lanes
                    else:
                        rs[there, :] = rs[there, :] + lanes
                    return total + (prod[:8] + prod[8:])

                return lax.fori_loop(0, T // 16, run, total)

            total = jnp.zeros((8, ZR), F32)
            total = part_of(res, pl.multiple_of(hcol + at, 128), 0, total)
            total = part_of(resp, at, T, total)
            ggt[:, pl.ds(at, ZR)] = jnp.sum(total, axis=0, keepdims=True)

        def input_grad(source, col, base):
            factor = 1.0 + gain_v[:, pl.ds(hcol, H)]

            def run(i, _):
                spot = pl.ds(pl.multiple_of(i * 16, 16), 16)
                there = pl.ds(pl.multiple_of(base + i * 16, 16), 16)
                scale = inv[there, :][:, :1]
                unit = source[spot, pl.ds(col, H)].astype(F32) * scale
                there_too = pl.ds(pl.multiple_of(T - base + i * 16, 16), 16)
                mean = jnp.sum(rs[there, :] + rsp[there_too, :], axis=1, keepdims=True) * (1.0 / D)
                ig[there, :] = (scale * (dn[there, :] * factor - unit * mean)).astype(BF16)
                return 0

            lax.fori_loop(0, T // 16, run, 0)

        delta_copy = pltpu.make_async_copy(od, delta_o, loc.at[6])
        ig_copy = pltpu.make_async_copy(ig.at[pl.ds(0, T)], igrad_o.at[0, :, pl.ds(hcol, H)], loc.at[7])
        values_copy = pltpu.make_async_copy(vout, values_o.at[0], loc.at[8])
        gain_copy = pltpu.make_async_copy(ggt, ggrad_o.at[:, pl.ds(hcol, H)], loc.at[9])

        def values_send():
            go(vacc.at[pl.ds(T, T)], vrecv, part_s.at[4], part_r.at[4], partner)

        def sums_send():
            go(rs, rsp, part_s.at[5], part_r.at[5], partner)
            ggx[x] = ggt[...]
            for k in range(1, 4):
                go(ggx.at[x], ggx.at[x], gx_s.at[k], gx_r.at[k], dev(q, (x + k) % 4, c))

        def igrad_other():
            got(rsp, part_r.at[5])
            input_grad(resp, 0, T)
            go(ig.at[pl.ds(T, T)], igrad_o.at[0, :, pl.ds(hcol, H)], part_s.at[6], part_r.at[6], partner)

        def igrad_own():
            input_grad(res, hcol, 0)
            ig_copy.start()

        def gain_x():
            for k in range(1, 4):
                got(ggx.at[(x + 4 - k) % 4], gx_r.at[k])
            ggz[q] = (ggx[0] + ggx[1]) + (ggx[2] + ggx[3])
            for k in range(1, 4):
                go(ggz.at[q], ggz.at[q], gz_s.at[k], gz_r.at[k], dev((q + k) % 4, x, c))

        def gain_z():
            for k in range(1, 4):
                got(ggz.at[(q + 4 - k) % 4], gz_r.at[k])
            ggt[...] = (ggz[0] + ggz[1]) + (ggz[2] + ggz[3])
            gain_copy.start()
            go(ggt, ggrad_o.at[:, pl.ds(hcol, H)], part_s.at[7], part_r.at[7], partner)

        def values_end():
            got(vrecv, part_r.at[4])
            vout[...] = ((vacc[pl.ds(0, T), :] + vrecv[...]) * out_scale).astype(BF16)
            values_copy.start()

        def delta_end():
            outer_out()
            delta_copy.start()

        steps = [
            own_in, lambda: ag_z_send(near, owner), lambda: ag_x_send(near, owner),
            ax_send, ax_left, ax_right, ax_end,
            lambda: ax_own(0), lambda: ax_own(1), lambda: ax_own(2), lambda: ax_own(3),
            scales, normed_own, normed_other,
            rx_opp, rx_right, rx_left, rx_end, grad_out,
            outer_start, outer_mid, outer_last, delta_end,
            values_send, sums_send, igrad_other, igrad_own, gain_x, gain_z, values_end,
        ]
        for zl, first in ((near, True), (far, False)):
            for run in (
                ag_z, ag_left, ag_right, ag_end, grad_rows, rs_opp,
                rs_right, rs_left, rs_x, rs_z, dnormed,
            ):
                steps.append(lambda run=run, zl=zl: run(zl))
            steps.append(lambda zl=zl, first=first: near_far_values(zl, first))
            steps.append(lambda zl=zl, first=first: sums(zl, first))
            for run in (ax_z, rx_z):
                for k in range(4):
                    steps.append(lambda run=run, zl=zl, k=k: run(zl, k))

        def finish():
            got(grad_o, part_r.at[8], not owner)
            got(igrad_o.at[0, :, pl.ds(pcol, H)], part_r.at[6])
            got(ggrad_o.at[:, pl.ds(pcol, H)], part_r.at[7])
            when(owner, lambda: grad_mine.wait())
            for item in (delta_copy, ig_copy, values_copy, gain_copy):
                item.wait()
            for cond, made in sends[first_sends:]:
                when(cond, lambda made=made: made.wait_send())

        for number in order:
            step(number, steps[number])
        step(-1, finish)
        del sends[first_sends:]

    for kind, order in enumerate(ORDERS):
        @pl.when(place == kind)
        def _(owner=kind < 2, order=order):
            all_steps(owner, order)

    for cond, made in sends:
        when(cond, lambda made=made: made.wait_send())


def main_call(frag, delay, residual, cotangent, gain, master, anchor, history):
    any_space = pl.BlockSpec(memory_space=pl.ANY)
    smem = pl.BlockSpec(memory_space=pltpu.SMEM)
    vm = pltpu.VMEM
    dma = pltpu.SemaphoreType.DMA
    nx = max(NX, 128)
    scratch = [
        vm((T, D), BF16), vm((T, H), BF16), vm((2 * T, DV), BF16), vm((1, D), F32),
        vm((R, DV), F32), vm((R, DV), F32), vm((HIST, PART, DV), F32),
        vm((H, DV), BF16), vm((R, DV), BF16), vm((H, DV), BF16), vm((2 * T, H), BF16),
        vm((2 * T, 128), F32), vm((2 * T, H), F32), vm((2 * T, DV), F32), vm((T, DV), F32),
        vm((T, DV), BF16), vm((2 * T, 128), F32), vm((2 * T, 128), F32), vm((2 * T, H), BF16),
        vm((4, 1, H), F32), vm((4, 1, H), F32), vm((1, H), F32),
        vm((2, 2, R, NZ), BF16), vm((2, 2, SLOT, NZ), BF16), vm((2, 2, SLOT, NZ), BF16),
        vm((2, 2, 4, SLOT, nx), BF16), vm((2, R, nx), BF16), vm((2, SLOT, nx), BF16),
        vm((PART, DV), F32), vm((4, PART, QUART), F32), vm((PART, QUART), F32),
        vm((PART, QUART), F32), vm((PART, DV), F32),
        dma((11,)), dma((9,)), dma((9,)), dma((2, 2)), dma((2,)), dma((2, 4)), dma((2, 4)),
        dma((4,)), dma((4,)), dma((2, 4, 2)), dma((2, 4)),
        dma((2, 4)), dma((2, 4)), dma((2, 2)), dma((2, 2)),
        dma((2, 2, 4)), dma((2, 2, 4)), dma((4,)), dma((4,)),
        dma((4,)), dma((4,)), dma((4,)), dma((4,)),
        dma((4,)), dma((4,)), dma, dma, dma((4,)), dma((4,)),
    ]
    return pl.pallas_call(
        main_kernel,
        out_shape=(
            jax.ShapeDtypeStruct((1, T, DV), BF16),
            jax.ShapeDtypeStruct((1, T, D), BF16),
            jax.ShapeDtypeStruct((1, D), F32),
            jax.ShapeDtypeStruct((R, DV), BF16),
            jax.ShapeDtypeStruct((PART, DV), F32),
        ),
        in_specs=[smem, smem] + [any_space] * 6,
        out_specs=(any_space,) * 5,
        scratch_shapes=scratch,
        compiler_params=pltpu.CompilerParams(
            collective_id=0, has_side_effects=True, vmem_limit_bytes=60 * 1024 * 1024
        ),
        name="inner_step",
    )(frag, delay, residual, cotangent, gain, master, anchor, history)


def update_kernel(
    frag, grad, delta, master, first, second, anchor, momentum, values, igrad, ggrad,
    master_o, first_o, second_o, anchor_o, momentum_o, values_o, igrad_o, ggrad_o,
    grad_v, delta_v, master_v, first_v, second_v, anchor_v, momentum_v,
    master_n, first_n, second_n, igrad_v, values_v, ggrad_v, load, load_small, store, through,
):
    rows = FRAGS * FR_ROWS
    groups = R // rows
    spots = [pl.ds(i * rows, rows) for i in range(groups)]
    small = [
        pltpu.make_async_copy(grad, grad_v, load_small.at[0]),
        pltpu.make_async_copy(delta, delta_v, load_small.at[1]),
    ]
    for item in small:
        item.start()
    loads = []
    for i, at in enumerate(spots):
        loads.append([
            pltpu.make_async_copy(src, dst, load.at[i, k])
            for k, (src, dst) in enumerate((
                (master.at[0, at], master_v.at[at]),
                (first.at[0, at], first_v.at[at]),
                (second.at[0, at], second_v.at[at]),
                (anchor.at[at], anchor_v.at[at]),
                (momentum.at[at], momentum_v.at[at]),
            ))
        ])
        for item in loads[-1]:
            item.start()
    half = T // 2
    taken, passed = [], []
    for k, (src, mid, dst) in enumerate((
        (igrad.at[0, :half], igrad_v.at[:half], igrad_o.at[0, :half]),
        (igrad.at[0, half:], igrad_v.at[half:], igrad_o.at[0, half:]),
        (values.at[0], values_v, values_o.at[0]),
        (ggrad, ggrad_v, ggrad_o),
    )):
        taken.append(pltpu.make_async_copy(src, mid, through.at[0, k]))
        passed.append(pltpu.make_async_copy(mid, dst, through.at[1, k]))
        taken[-1].start()
    for item in small:
        item.wait()
    begin = lax.axis_index("fsdp") * (R // FR_ROWS)
    stores = []
    for i, at in enumerate(spots):
        for item in loads[i]:
            item.wait()
        chosen = jnp.int32(0)
        for k in range(1, FRAGS):
            chosen = chosen + jnp.where(frag[begin + i * FRAGS + k] == 0, k, 0)
        block = pl.ds(pl.multiple_of(i * rows + chosen * FR_ROWS, FR_ROWS), FR_ROWS)

        for piece in range(rows // 16):
            part = pl.ds(i * rows + piece * 16, 16)
            gradient = grad_v[part, :].astype(F32)
            weights = master_v[part, :]
            first_new = beta_one * first_v[part, :] + (1.0 - beta_one) * gradient
            second_new = beta_two * second_v[part, :] + (1.0 - beta_two) * gradient * gradient
            first_n[part, :] = first_new
            second_n[part, :] = second_new
            master_n[part, :] = weights - inner_rate * (
                first_new / (jnp.sqrt(second_new) + adam_eps) + weight_decay * weights
            )
        change = delta_v[pl.ds(i * FR_ROWS, FR_ROWS), :]
        anchor_old = anchor_v[block, :]
        momentum_part = outer_beta * momentum_v[block, :] + change
        anchor_part = anchor_old - outer_rate * (change + outer_beta * momentum_part)
        anchor_v[block, :] = anchor_part
        momentum_v[block, :] = momentum_part
        master_n[block, :] = mix_weight * master_n[block, :] + (1.0 - mix_weight) * anchor_part
        for k, (src, dst) in enumerate((
            (master_n.at[at], master_o.at[0, at]),
            (first_n.at[at], first_o.at[0, at]),
            (second_n.at[at], second_o.at[0, at]),
            (anchor_v.at[at], anchor_o.at[at]),
            (momentum_v.at[at], momentum_o.at[at]),
        )):
            item = pltpu.make_async_copy(src, dst, store.at[i, k])
            item.start()
            stores.append(item)
        if i == 0:
            for came, goes in zip(taken, passed):
                came.wait()
                goes.start()
    for item in stores + passed:
        item.wait()


def update_call(frag, grad, delta, master, first, second, anchor, momentum, values, igrad, ggrad):
    any_space = pl.BlockSpec(memory_space=pl.ANY)
    like3 = jax.ShapeDtypeStruct((1, R, DV), F32)
    like2 = jax.ShapeDtypeStruct((R, DV), F32)
    dma = pltpu.SemaphoreType.DMA
    whole = pltpu.VMEM((R, DV), F32)
    groups = R // (FRAGS * FR_ROWS)
    return pl.pallas_call(
        update_kernel,
        out_shape=(
            like3, like3, like3, like2, like2,
            jax.ShapeDtypeStruct((1, T, DV), BF16),
            jax.ShapeDtypeStruct((1, T, D), BF16),
            jax.ShapeDtypeStruct((1, D), F32),
        ),
        in_specs=[pl.BlockSpec(memory_space=pltpu.SMEM)] + [any_space] * 10,
        out_specs=(any_space,) * 8,
        scratch_shapes=[pltpu.VMEM((R, DV), BF16), pltpu.VMEM((PART, DV), F32)]
        + [whole] * 8
        + [pltpu.VMEM((T, D), BF16), pltpu.VMEM((T, DV), BF16), pltpu.VMEM((1, D), F32)]
        + [dma((groups, 5)), dma((2,)), dma((groups, 5)), dma((2, 4))],
        compiler_params=pltpu.CompilerParams(vmem_limit_bytes=60 * 1024 * 1024),
        name="update",
    )(frag, grad, delta, master, first, second, anchor, momentum, values, igrad, ggrad)


def body(
    residual, cotangent, norm_gain, master, first_moment, second_moment,
    anchor, outer_momentum, history, fragment, delay,
):
    values, input_grad, gain_grad, gradient, delta = main_call(
        fragment, delay, residual, cotangent, norm_gain, master, anchor, history
    )
    new_master, new_first, new_second, new_anchor, new_momentum, values, input_grad, gain_grad = update_call(
        fragment, gradient, delta, master, first_moment, second_moment, anchor, outer_momentum,
        values, input_grad, gain_grad,
    )
    return (
        values, input_grad, gain_grad, new_master, new_first, new_second, new_anchor, new_momentum,
    )


def solution(mesh):
    rows = P("replica", "fsdp", None)
    both = P("fsdp", None)
    return jax.shard_map(
        body,
        mesh=mesh,
        in_specs=(
            rows, rows, P("replica", None), rows, rows, rows, both, both,
            P("replica", None, "fsdp", None), P(), P("replica", "fsdp"),
        ),
        out_specs=(rows, rows, P("replica", None), rows, rows, rows, both, both),
        check_vma=False,
    )
```

time: 265 us -> 85.4 us (0.32)
  the two profiles are of different devices: /device:TPU:16 before, /device:TPU:1 now
where the time goes in v2:
time: 85.4 us; the launch traced here: 85.3 us
  Pallas kernels  84.4 us (99%)
    pallas_call x1, Pallas kernels, main_call(): pl.pallas_call(main_kernel, out_shape=(jax.ShapeDtypeStruct((1, T, DV), B...  77.9 us
    pallas_call x1, Pallas kernels, update_call(): pl.pallas_call(update_kernel, out_shape=(like3, like3, like3, like2, like...  6.58 us

profile of v2, /device:TPU:1, one launch (start us, length us, event | category | flops | bytes accessed | tf_op | source)
XLA Modules:
  0.0 85.3 jit_solution(14724558336497362665)
XLA Ops:
  0.6 77.9 %inner_step.1 = (bf16[1,256,1024]{2,1,0:T(8,128)(2,1)}, bf16[1,256,4608]{2,1,0:T(8,128)(2,1)}, f32[1,4608]{1,0:T(1,128)}, bf16[144,1024]{1,0:T(8,128)(2,1)}, f32[24,1024]{1,0:T(8,128)}) custom-call(s32[576]{0:T(1024)} %frag.3, s32[1,3]{1,0:T(1,128)} %delay.1, bf16[1,256,4608]{2,1,0:T(8,128)(2,1)} %residual.1, bf16[1,256,1024]{2,1,0:T(8,128)(2,1)} %cotangent.1, ...), custom_call_target="tpu_custom_call" | custom-call | tf_op jit(solution)/shard_map/inner_step/pallas_call | solution.py:602
  78.5 6.6 %update.1 = (f32[1,144,1024]{2,1,0:T(8,128)}, f32[1,144,1024]{2,1,0:T(8,128)}, f32[1,144,1024]{2,1,0:T(8,128)}, f32[144,1024]{1,0:T(8,128)}, f32[144,1024]{1,0:T...) custom-call(s32[576]{0:T(1024)} %frag.3, ...), custom_call_target="tpu_custom_call" | custom-call | tf_op jit(solution)/shard_map/update/pallas_call | solution.py:716

commit v3 on v2

--- a/solution.py
+++ b/solution.py
@@ -40,24 +40,26 @@
 
 ORDERS = [
     [
-        0, 1, 3, 11, 7, 2, 5, 4, 8, 51, 31, 6, 32, 10, 9, 53, 13, 33, 19, 12, 65, 52, 66, 67, 20, 64, 54, 40,
-        34, 55, 56, 68, 70, 61, 41, 71, 69, 21, 35, 42, 63, 57, 58, 24, 36, 48, 37, 22, 62, 47, 49, 59, 27,
-        50, 14, 60, 23, 15, 16, 25, 29, 26, 38, 28, 39, 17, 18,
+        1, 5, 0, 10, 6, 4, 14, 3, 2, 60, 8, 12, 7, 11, 61, 37, 38, 9, 78, 13, 16, 39, 15, 77, 79, 24, 62, 63,
+        50, 49, 80, 65, 64, 40, 51, 82, 25, 84, 66, 74, 81, 68, 41, 83, 26, 67, 76, 69, 75, 29, 42, 27, 44,
+        70, 56, 43, 57, 71, 32, 73, 72, 58, 59, 17, 30, 28, 18, 19, 20, 46, 31, 33, 48, 34, 45, 47, 22, 21,
+        23,
     ],
     [
-        0, 1, 3, 11, 2, 7, 4, 8, 5, 12, 51, 32, 64, 6, 13, 31, 65, 10, 19, 9, 20, 67, 33, 66, 34, 53, 52, 55,
-        40, 41, 56, 54, 42, 61, 69, 57, 68, 58, 21, 35, 47, 62, 70, 63, 71, 50, 59, 24, 49, 48, 14, 37, 23,
-        36, 25, 60, 15, 16, 27, 26, 38, 22, 17, 29, 39, 18, 28,
+        1, 5, 24, 0, 6, 2, 10, 4, 60, 8, 7, 11, 3, 14, 12, 61, 16, 78, 15, 37, 38, 9, 25, 13, 77, 79, 40, 39,
+        65, 50, 62, 63, 80, 49, 64, 74, 66, 67, 51, 83, 75, 81, 69, 82, 68, 41, 76, 28, 42, 26, 29, 84, 56,
+        57, 58, 30, 59, 17, 71, 70, 44, 43, 18, 73, 32, 31, 72, 20, 19, 27, 34, 45, 46, 47, 48, 33, 22, 21,
+        23,
     ],
     [
-        11, 13, 12, 30, 43, 55, 34, 51, 65, 56, 19, 35, 45, 32, 71, 52, 68, 69, 70, 31, 53, 58, 46, 64, 20,
-        57, 44, 67, 37, 66, 47, 50, 36, 33, 49, 54, 48, 21, 40, 42, 59, 61, 63, 38, 60, 41, 24, 62, 39, 23,
-        25, 27, 22, 26, 28, 29,
+        14, 35, 15, 16, 36, 65, 60, 53, 40, 54, 67, 61, 37, 52, 66, 38, 55, 83, 78, 63, 69, 77, 81, 41, 62,
+        39, 24, 58, 68, 79, 82, 57, 49, 42, 80, 51, 84, 50, 43, 44, 56, 25, 71, 59, 64, 73, 74, 76, 45, 70,
+        26, 29, 46, 75, 72, 47, 28, 30, 48, 32, 33, 27, 34, 31,
     ],
     [
-        11, 19, 13, 12, 55, 68, 56, 69, 34, 71, 70, 58, 35, 48, 50, 57, 49, 47, 30, 43, 51, 20, 32, 45, 31,
-        36, 59, 60, 37, 44, 46, 53, 21, 65, 52, 33, 64, 40, 41, 38, 42, 22, 67, 39, 66, 54, 61, 63, 24, 62,
-        23, 25, 27, 29, 28, 26,
+        14, 15, 16, 40, 41, 65, 66, 83, 84, 24, 35, 25, 57, 43, 69, 81, 36, 58, 82, 67, 68, 56, 38, 54, 60,
+        37, 59, 61, 71, 26, 73, 44, 55, 53, 39, 52, 27, 42, 63, 49, 62, 70, 77, 51, 50, 46, 72, 45, 64, 47,
+        79, 48, 78, 80, 74, 76, 29, 75, 30, 32, 31, 28, 33, 34,
     ],
 ]
 
@@ -135,6 +137,19 @@
     greeted += [{"replica": y * 2 + 1 - zh}]
     for to in greeted:
         pl.semaphore_signal(barrier, inc=1, device_id=to, device_id_type=MESH)
+
+    own = q % 2
+    local_in[0].wait()
+    own_rows = pl.ds(pl.multiple_of(own * ZR + x * SLOT + c * R, 16), R)
+
+    @pl.when(handler)
+    def _():
+        wh[own_rows, :] = master_v[...].astype(BF16)
+
+    @pl.when(jnp.logical_not(handler))
+    def _():
+        stage[...] = master_v[...].astype(BF16)
+
     pl.semaphore_wait(barrier, len(greeted))
 
     zcols, xcols = pl.ds(0, NZ), pl.ds(NZ, NX)
@@ -150,18 +165,6 @@
     hcol = pl.multiple_of(c * H, 128)
     pcol = pl.multiple_of((1 - c) * H, 128)
 
-    own = q % 2
-    local_in[0].wait()
-    own_rows = pl.ds(pl.multiple_of(own * ZR + x * SLOT + c * R, 16), R)
-
-    @pl.when(handler)
-    def _():
-        wh[own_rows, :] = master_v[...].astype(BF16)
-
-    @pl.when(jnp.logical_not(handler))
-    def _():
-        stage[...] = master_v[...].astype(BF16)
-
     go(stage, wh.at[own_rows, :], part_s.at[0], part_r.at[0], partner, jnp.logical_not(handler))
     other_rows = pl.ds(pl.multiple_of(own * ZR + x * SLOT + (1 - c) * R, 16), R)
 
@@ -184,55 +187,60 @@
         def own_in():
             got(wh.at[other_rows, :], part_r.at[0], owner)
 
-        def ag_z_send(zl, cond):
-            ref = block(wh, zl, x, zcols)
+        def turn(h):
+            return c if h == 0 else 1 - c
+
+        def ag_z_send(zl, h, cond):
+            ref = block(wh, zl, x, zcols, turn(h))
             go_up, go_down = towards(zl)
-            go(ref, ref, agz_s.at[zl, 0], agz_r.at[zl], up, both(cond, go_up))
-            go(ref, ref, agz_s.at[zl, 1], agz_r.at[zl], down, both(cond, go_down))
-
-        def ag_x_send(zl, cond):
-            ref = block(wh, zl, x, zcols)
-            go(ref, ref, agx_s.at[zl, 0], agx_r.at[zl, 0], right, cond)
-            go(ref, ref, agx_s.at[zl, 1], agx_r.at[zl, 1], left, cond)
-
-        def ag_z(zl):
+            go(ref, ref, agz_s.at[zl, 0, h], agz_r.at[zl, h], up, both(cond, go_up))
+            go(ref, ref, agz_s.at[zl, 1, h], agz_r.at[zl, h], down, both(cond, go_down))
+
+        def ag_x_send(zl, h, cond):
+            ref = block(wh, zl, x, zcols, turn(h))
+            go(ref, ref, agx_s.at[zl, turn(h)], agx_r.at[zl, turn(h)], right, cond)
+            go(ref, ref, agx_s.at[zl, 2 + turn(h)], agx_r.at[zl, 2 + turn(h)], left, cond)
+
+        def ag_z(zl, h):
             cond = not (owner and zl is near)
-            got(block(wh, zl, x, zcols), agz_r.at[zl], cond)
-            ag_z_send(zl, cond)
-            ag_x_send(zl, cond)
+            got(block(wh, zl, x, zcols, turn(h)), agz_r.at[zl, h], cond)
+            ag_z_send(zl, h, cond)
+            ag_x_send(zl, h, cond)
 
         def ag_left(zl):
-            got(block(wh, zl, xl, zcols), agx_r.at[zl, 0])
             ref = block(wh, zl, xl, zcols, 0)
-            go(ref, ref, agx_s.at[zl, 2], agx_r.at[zl, 2], right)
+            got(ref, agx_r.at[zl, 0])
+            go(ref, ref, agx_s.at[zl, 4], agx_r.at[zl, 4], right)
 
         def ag_right(zl):
-            got(block(wh, zl, xr, zcols), agx_r.at[zl, 1])
             ref = block(wh, zl, xr, zcols, 1)
-            go(ref, ref, agx_s.at[zl, 3], agx_r.at[zl, 3], left)
+            got(ref, agx_r.at[zl, 3])
+            go(ref, ref, agx_s.at[zl, 5], agx_r.at[zl, 5], left)
 
         def ag_end(zl):
-            got(block(wh, zl, xo, zcols, 0), agx_r.at[zl, 2])
-            got(block(wh, zl, xo, zcols, 1), agx_r.at[zl, 3])
-
-        def ax_send():
-            ref = block(wh, own, x, xcols)
-            go(ref, ref, axx_s.at[0], axx_r.at[0], right, owner)
-            go(ref, ref, axx_s.at[1], axx_r.at[1], left, owner)
+            got(block(wh, zl, xl, zcols, 1), agx_r.at[zl, 1])
+            got(block(wh, zl, xr, zcols, 0), agx_r.at[zl, 2])
+            got(block(wh, zl, xo, zcols, 0), agx_r.at[zl, 4])
+            got(block(wh, zl, xo, zcols, 1), agx_r.at[zl, 5])
+
+        def ax_send(h):
+            ref = block(wh, own, x, xcols, turn(h))
+            go(ref, ref, axx_s.at[h], axx_r.at[h], right, owner)
+            go(ref, ref, axx_s.at[2 + h], axx_r.at[2 + h], left, owner)
 
         def ax_left():
-            got(block(wh, own, xl, xcols), axx_r.at[0], owner)
             ref = block(wh, own, xl, xcols, 0)
-            go(ref, ref, axx_s.at[2], axx_r.at[2], right, owner)
+            got(ref, axx_r.at[c], owner)
+            go(ref, ref, axx_s.at[4], axx_r.at[4], right, owner)
 
         def ax_right():
-            got(block(wh, own, xr, xcols), axx_r.at[1], owner)
             ref = block(wh, own, xr, xcols, 1)
-            go(ref, ref, axx_s.at[3], axx_r.at[3], left, owner)
+            got(ref, axx_r.at[3 - c], owner)
+            go(ref, ref, axx_s.at[5], axx_r.at[5], left, owner)
 
         def ax_end():
-            got(block(wh, own, xo, xcols, 0), axx_r.at[2], owner)
-            got(block(wh, own, xo, xcols, 1), axx_r.at[3], owner)
+            got(block(wh, own, xo, xcols, 0), axx_r.at[4], owner)
+            got(block(wh, own, xo, xcols, 1), axx_r.at[5], owner)
 
         def ax_z_send(zl, k, cond):
             ref = block(wh, zl, slot_of(k), xcols)
@@ -241,6 +249,10 @@
             go(ref, ref, axz_s.at[zl, k, 1], axz_r.at[zl, k], down, both(cond, go_down))
 
         def ax_own(k):
+            if k == 1:
+                got(block(wh, own, xl, xcols, 1), axx_r.at[1 - c], owner)
+            if k == 2:
+                got(block(wh, own, xr, xcols, 0), axx_r.at[2 + c], owner)
             ax_z_send(near, k, owner)
 
         def ax_z(zl, k):
@@ -311,31 +323,40 @@
             go(block(g, zl, xo, zcols, 0), opp.at[zl, 0], rsx_s.at[zl, 0], rsx_r.at[zl, 0], right)
             go(block(g, zl, xo, zcols, 1), opp.at[zl, 1], rsx_s.at[zl, 1], rsx_r.at[zl, 1], left)
 
+        first_half, second_half = pl.ds(0, R), pl.ds(R, R)
+
+        def rs_plain(zl):
+            go(block(g, zl, xr, zcols, 1), full.at[zl, 0, second_half], rsx_s.at[zl, 4], rsx_r.at[zl, 4], right)
+            go(block(g, zl, xl, zcols, 0), full.at[zl, 1, first_half], rsx_s.at[zl, 5], rsx_r.at[zl, 5], left)
+
         def rs_right(zl):
             got(opp.at[zl, 0], rsx_r.at[zl, 0])
             add_into(rows(zl, xr, 0), R, zcols, [opp.at[zl, 0]])
-            go(block(g, zl, xr, zcols), full.at[zl, 0], rsx_s.at[zl, 2], rsx_r.at[zl, 2], right)
+            go(block(g, zl, xr, zcols, 0), full.at[zl, 0, first_half], rsx_s.at[zl, 2], rsx_r.at[zl, 2], right)
 
         def rs_left(zl):
             got(opp.at[zl, 1], rsx_r.at[zl, 1])
             add_into(rows(zl, xl, 1), R, zcols, [opp.at[zl, 1]])
-            go(block(g, zl, xl, zcols), full.at[zl, 1], rsx_s.at[zl, 3], rsx_r.at[zl, 3], left)
-
-        def rs_x(zl):
-            got(full.at[zl, 0], rsx_r.at[zl, 2])
-            got(full.at[zl, 1], rsx_r.at[zl, 3])
-            add_into(rows(zl, x), SLOT, zcols, [full.at[zl, 0], full.at[zl, 1]])
-
-        def rs_z(zl):
+            go(block(g, zl, xl, zcols, 1), full.at[zl, 1, second_half], rsx_s.at[zl, 3], rsx_r.at[zl, 3], left)
+
+        def rs_x(zl, h):
+            part = (first_half, second_half)[h]
+            got(full.at[zl, 0, part], rsx_r.at[zl, (2, 4)[h]])
+            got(full.at[zl, 1, part], rsx_r.at[zl, (5, 3)[h]])
+            add_into(rows(zl, x, h), R, zcols, [full.at[zl, 0, part], full.at[zl, 1, part]])
+
+        def rs_z(zl, h):
             above, below = towards(zl)
-            got(zbuf.at[zl, 1], rsz_r.at[zl, 1], above)
-            add_into(rows(zl, x), SLOT, zcols, [zbuf.at[zl, 1]], above)
-            got(zbuf.at[zl, 0], rsz_r.at[zl, 0], below)
-            add_into(rows(zl, x), SLOT, zcols, [zbuf.at[zl, 0]], below)
-            ref = block(g, zl, x, zcols)
             goal = 2 * c + zl
-            go(ref, zbuf.at[zl, 1], rsz_s.at[zl, 0], rsz_r.at[zl, 1], down, q > goal)
-            go(ref, zbuf.at[zl, 0], rsz_s.at[zl, 1], rsz_r.at[zl, 0], up, q < goal)
+            high = zbuf.at[zl, 1, pl.ds(h * R, R)]
+            low = zbuf.at[zl, 0, pl.ds(h * R, R)]
+            got(high, rsz_r.at[zl, 1, h], above)
+            add_into(rows(zl, x, h), R, zcols, [high], above)
+            got(low, rsz_r.at[zl, 0, h], below)
+            add_into(rows(zl, x, h), R, zcols, [low], below)
+            ref = block(g, zl, x, zcols, h)
+            go(ref, high, rsz_s.at[zl, 0, h], rsz_r.at[zl, 1, h], down, q > goal)
+            go(ref, low, rsz_s.at[zl, 1, h], rsz_r.at[zl, 0, h], up, q < goal)
 
         def rx_z(zl, k):
             above, below = towards(zl)
@@ -353,26 +374,35 @@
             go(block(g, own, xo, xcols, 0), oppx.at[0], rxx_s.at[0], rxx_r.at[0], right, owner)
             go(block(g, own, xo, xcols, 1), oppx.at[1], rxx_s.at[1], rxx_r.at[1], left, owner)
 
+        def rx_plain():
+            go(block(g, own, xr, xcols, 1), fullx.at[0, second_half], rxx_s.at[4], rxx_r.at[4], right, owner)
+            go(block(g, own, xl, xcols, 0), fullx.at[1, first_half], rxx_s.at[5], rxx_r.at[5], left, owner)
+
         def rx_right():
             got(oppx.at[0], rxx_r.at[0], owner)
             add_into(rows(own, xr, 0), R, xcols, [oppx.at[0]], owner)
-            go(block(g, own, xr, xcols), fullx.at[0], rxx_s.at[2], rxx_r.at[2], right, owner)
+            go(block(g, own, xr, xcols, 0), fullx.at[0, first_half], rxx_s.at[2], rxx_r.at[2], right, owner)
 
         def rx_left():
             got(oppx.at[1], rxx_r.at[1], owner)
             add_into(rows(own, xl, 1), R, xcols, [oppx.at[1]], owner)
-            go(block(g, own, xl, xcols), fullx.at[1], rxx_s.at[3], rxx_r.at[3], left, owner)
+            go(block(g, own, xl, xcols, 1), fullx.at[1, second_half], rxx_s.at[3], rxx_r.at[3], left, owner)
 
         def rx_end():
-            got(fullx.at[0], rxx_r.at[2], owner)
-            got(fullx.at[1], rxx_r.at[3], owner)
-            add_into(rows(own, x), SLOT, xcols, [fullx.at[0], fullx.at[1]], owner)
-
-        grad_mine = pltpu.make_async_copy(g.at[own_rows, :], grad_o, loc.at[10])
-
-        def grad_out():
-            when(owner, lambda: grad_mine.start())
-            go(g.at[other_rows, :], grad_o, part_s.at[8], part_r.at[8], partner, owner)
+            for h, part in ((0, first_half), (1, second_half)):
+                got(fullx.at[0, part], rxx_r.at[(2, 4)[h]], owner)
+                got(fullx.at[1, part], rxx_r.at[(5, 3)[h]], owner)
+                add_into(rows(own, x, h), R, xcols, [fullx.at[0, part], fullx.at[1, part]], owner)
+
+        grad_mine = [
+            pltpu.make_async_copy(g.at[own_rows, cols], grad_o.at[:, cols], loc.at[10 + k])
+            for k, cols in enumerate((zcols, xcols))
+        ]
+
+        def grad_out(k):
+            cols = (zcols, xcols)[k]
+            when(owner, lambda: grad_mine[k].start())
+            go(g.at[other_rows, cols], grad_o.at[:, cols], part_s.at[8 + k], part_r.at[8 + k], partner, owner)
 
         def outer_start():
             local_in[4].wait()
@@ -531,20 +561,27 @@
             delta_copy.start()
 
         steps = [
-            own_in, lambda: ag_z_send(near, owner), lambda: ag_x_send(near, owner),
-            ax_send, ax_left, ax_right, ax_end,
+            own_in, lambda: ag_z_send(near, 0, owner), lambda: ag_z_send(near, 1, owner),
+            lambda: ag_x_send(near, 0, owner), lambda: ag_x_send(near, 1, owner),
+            lambda: ax_send(0), lambda: ax_send(1), ax_left, ax_right, ax_end,
             lambda: ax_own(0), lambda: ax_own(1), lambda: ax_own(2), lambda: ax_own(3),
             scales, normed_own, normed_other,
-            rx_opp, rx_right, rx_left, rx_end, grad_out,
+            rx_opp, rx_plain, rx_right, rx_left, rx_end, lambda: grad_out(0), lambda: grad_out(1),
             outer_start, outer_mid, outer_last, delta_end,
             values_send, sums_send, igrad_other, igrad_own, gain_x, gain_z, values_end,
         ]
         for zl, first in ((near, True), (far, False)):
+            steps.append(lambda zl=zl: ag_z(zl, 0))
+            steps.append(lambda zl=zl: ag_z(zl, 1))
             for run in (
-                ag_z, ag_left, ag_right, ag_end, grad_rows, rs_opp,
-                rs_right, rs_left, rs_x, rs_z, dnormed,
+                ag_left, ag_right, ag_end, grad_rows, rs_opp,
+                rs_plain, rs_right, rs_left,
             ):
                 steps.append(lambda run=run, zl=zl: run(zl))
+            for run in (rs_x, rs_z):
+                steps.append(lambda run=run, zl=zl: run(zl, 0))
+                steps.append(lambda run=run, zl=zl: run(zl, 1))
+            steps.append(lambda zl=zl: dnormed(zl))
             steps.append(lambda zl=zl, first=first: near_far_values(zl, first))
             steps.append(lambda zl=zl, first=first: sums(zl, first))
             for run in (ax_z, rx_z):
@@ -552,10 +589,12 @@
                     steps.append(lambda run=run, zl=zl, k=k: run(zl, k))
 
         def finish():
-            got(grad_o, part_r.at[8], not owner)
+            for k, cols in enumerate((zcols, xcols)):
+                got(grad_o.at[:, cols], part_r.at[8 + k], not owner)
             got(igrad_o.at[0, :, pl.ds(pcol, H)], part_r.at[6])
             got(ggrad_o.at[:, pl.ds(pcol, H)], part_r.at[7])
-            when(owner, lambda: grad_mine.wait())
+            for item in grad_mine:
+                when(owner, lambda item=item: item.wait())
             for item in (delta_copy, ig_copy, values_copy, gain_copy):
                 item.wait()
             for cond, made in sends[first_sends:]:
@@ -592,10 +631,10 @@
         vm((2, 2, 4, SLOT, nx), BF16), vm((2, R, nx), BF16), vm((2, SLOT, nx), BF16),
         vm((PART, DV), F32), vm((4, PART, QUART), F32), vm((PART, QUART), F32),
         vm((PART, QUART), F32), vm((PART, DV), F32),
-        dma((11,)), dma((9,)), dma((9,)), dma((2, 2)), dma((2,)), dma((2, 4)), dma((2, 4)),
-        dma((4,)), dma((4,)), dma((2, 4, 2)), dma((2, 4)),
-        dma((2, 4)), dma((2, 4)), dma((2, 2)), dma((2, 2)),
-        dma((2, 2, 4)), dma((2, 2, 4)), dma((4,)), dma((4,)),
+        dma((12,)), dma((10,)), dma((10,)), dma((2, 2, 2)), dma((2, 2)), dma((2, 6)), dma((2, 6)),
+        dma((6,)), dma((6,)), dma((2, 4, 2)), dma((2, 4)),
+        dma((2, 6)), dma((2, 6)), dma((2, 2, 2)), dma((2, 2, 2)),
+        dma((2, 2, 4)), dma((2, 2, 4)), dma((6,)), dma((6,)),
         dma((4,)), dma((4,)), dma((4,)), dma((4,)),
         dma((4,)), dma((4,)), dma, dma, dma((4,)), dma((4,)),
     ]
@@ -612,7 +651,7 @@
         out_specs=(any_space,) * 5,
         scratch_shapes=scratch,
         compiler_params=pltpu.CompilerParams(
-            collective_id=0, has_side_effects=True, vmem_limit_bytes=60 * 1024 * 1024
+            collective_id=0, has_side_effects=True, vmem_limit_bytes=44 * 1024 * 1024
         ),
         name="inner_step",
     )(frag, delay, residual, cotangent, gain, master, anchor, history)
@@ -622,7 +661,7 @@
     frag, grad, delta, master, first, second, anchor, momentum, values, igrad, ggrad,
     master_o, first_o, second_o, anchor_o, momentum_o, values_o, igrad_o, ggrad_o,
     grad_v, delta_v, master_v, first_v, second_v, anchor_v, momentum_v,
-    master_n, first_n, second_n, igrad_v, values_v, ggrad_v, load, load_small, store, through,
+    master_n, first_n, second_n, load, load_small, stored, through,
 ):
     rows = FRAGS * FR_ROWS
     groups = R // rows
@@ -645,19 +684,14 @@
                 (momentum.at[at], momentum_v.at[at]),
             ))
         ])
-        for item in loads[-1]:
-            item.start()
-    half = T // 2
-    taken, passed = [], []
-    for k, (src, mid, dst) in enumerate((
-        (igrad.at[0, :half], igrad_v.at[:half], igrad_o.at[0, :half]),
-        (igrad.at[0, half:], igrad_v.at[half:], igrad_o.at[0, half:]),
-        (values.at[0], values_v, values_o.at[0]),
-        (ggrad, ggrad_v, ggrad_o),
-    )):
-        taken.append(pltpu.make_async_copy(src, mid, through.at[0, k]))
-        passed.append(pltpu.make_async_copy(mid, dst, through.at[1, k]))
-        taken[-1].start()
+    for item in loads[0] + loads[1] + loads[2]:
+        item.start()
+    passed = [
+        pltpu.make_async_copy(src, dst, through.at[k])
+        for k, (src, dst) in enumerate(((igrad, igrad_o), (values, values_o), (ggrad, ggrad_o)))
+    ]
+    for item in passed:
+        item.start()
     for item in small:
         item.wait()
     begin = lax.axis_index("fsdp") * (R // FR_ROWS)
@@ -670,6 +704,20 @@
             chosen = chosen + jnp.where(frag[begin + i * FRAGS + k] == 0, k, 0)
         block = pl.ds(pl.multiple_of(i * rows + chosen * FR_ROWS, FR_ROWS), FR_ROWS)
 
+        change = delta_v[pl.ds(i * FR_ROWS, FR_ROWS), :]
+        anchor_old = anchor_v[block, :]
+        momentum_part = outer_beta * momentum_v[block, :] + change
+        anchor_part = anchor_old - outer_rate * (change + outer_beta * momentum_part)
+        anchor_v[block, :] = anchor_part
+        momentum_v[block, :] = momentum_part
+
+        def store(k, src, dst):
+            item = pltpu.make_async_copy(src, dst, stored.at[i, k])
+            item.start()
+            stores.append(item)
+
+        store(0, anchor_v.at[at], anchor_o.at[at])
+        store(1, momentum_v.at[at], momentum_o.at[at])
         for piece in range(rows // 16):
             part = pl.ds(i * rows + piece * 16, 16)
             gradient = grad_v[part, :].astype(F32)
@@ -681,27 +729,10 @@
             master_n[part, :] = weights - inner_rate * (
                 first_new / (jnp.sqrt(second_new) + adam_eps) + weight_decay * weights
             )
-        change = delta_v[pl.ds(i * FR_ROWS, FR_ROWS), :]
-        anchor_old = anchor_v[block, :]
-        momentum_part = outer_beta * momentum_v[block, :] + change
-        anchor_part = anchor_old - outer_rate * (change + outer_beta * momentum_part)
-        anchor_v[block, :] = anchor_part
-        momentum_v[block, :] = momentum_part
+        store(2, first_n.at[at], first_o.at[0, at])
+        store(3, second_n.at[at], second_o.at[0, at])
         master_n[block, :] = mix_weight * master_n[block, :] + (1.0 - mix_weight) * anchor_part
-        for k, (src, dst) in enumerate((
-            (master_n.at[at], master_o.at[0, at]),
-            (first_n.at[at], first_o.at[0, at]),
-            (second_n.at[at], second_o.at[0, at]),
-            (anchor_v.at[at], anchor_o.at[at]),
-            (momentum_v.at[at], momentum_o.at[at]),
-        )):
-            item = pltpu.make_async_copy(src, dst, store.at[i, k])
-            item.start()
-            stores.append(item)
-        if i == 0:
-            for came, goes in zip(taken, passed):
-                came.wait()
-                goes.start()
+        store(4, master_n.at[at], master_o.at[0, at])
     for item in stores + passed:
         item.wait()
 
@@ -725,9 +756,8 @@
         out_specs=(any_space,) * 8,
         scratch_shapes=[pltpu.VMEM((R, DV), BF16), pltpu.VMEM((PART, DV), F32)]
         + [whole] * 8
-        + [pltpu.VMEM((T, D), BF16), pltpu.VMEM((T, DV), BF16), pltpu.VMEM((1, D), F32)]
-        + [dma((groups, 5)), dma((2,)), dma((groups, 5)), dma((2, 4))],
-        compiler_params=pltpu.CompilerParams(vmem_limit_bytes=60 * 1024 * 1024),
+        + [dma((groups, 5)), dma((2,)), dma((groups, 5)), dma((3,))],
+        compiler_params=pltpu.CompilerParams(vmem_limit_bytes=16 * 1024 * 1024),
         name="update",
     )(frag, grad, delta, master, first, second, anchor, momentum, values, igrad, ggrad)
 
@@ -736,6 +766,16 @@
     residual, cotangent, norm_gain, master, first_moment, second_moment,
     anchor, outer_momentum, history, fragment, delay,
 ):
+    (
+        residual, cotangent, norm_gain, master, first_moment, second_moment,
+        anchor, outer_momentum, history, fragment, delay,
+    ) = [
+        pltpu.with_memory_space_constraint(item, pltpu.HBM)
+        for item in (
+            residual, cotangent, norm_gain, master, first_moment, second_moment,
+            anchor, outer_momentum, history, fragment, delay,
+        )
+    ]
     values, input_grad, gain_grad, gradient, delta = main_call(
         fragment, delay, residual, cotangent, norm_gain, master, anchor, history
     )

time: 85.4 us -> 81.6 us (0.956)
  Pallas kernels: 84.4 us -> 80.5 us
    pallas_call x1, Pallas kernels: 77.9 us -> 75.4 us  [main_call(): pl.pallas_call(main_kernel, out_shape=(jax.ShapeDtypeStruct((1, T, DV), B...]
    pallas_call x1, Pallas kernels: 6.58 us -> 5.14 us  [update_call(): pl.pallas_call(update_kernel, out_shape=(like3, like3, like3, like2, like...]
where the time goes in v3:
time: 81.6 us; the launch traced here: 81.4 us
  Pallas kernels  80.5 us (99%)
  between operations  0.82 us (1%)
    pallas_call x1, Pallas kernels, main_call(): pl.pallas_call(main_kernel, out_shape=(jax.ShapeDtypeStruct((1, T, DV), B...  75.4 us
    pallas_call x1, Pallas kernels, update_call(): pl.pallas_call(update_kernel, out_shape=(like3, like3, like3, like2, like...  5.14 us

profile of v3, /device:TPU:1, one launch (start us, length us, event | category | flops | bytes accessed | tf_op | source)
XLA Modules:
  0.0 81.4 jit_solution(53157846796264613)
XLA Ops:
  0.6 75.4 %inner_step.1 = (bf16[1,256,1024]{2,1,0:T(8,128)(2,1)S(1)}, bf16[1,256,4608]{2,1,0:T(8,128)(2,1)S(1)}, f32[1,4608]{1,0:T(1,128)S(1)}, bf16[144,1024]{1,0:T(8,128)(2,1)S(1)}, f32[24,1024]{1,0:T(8,128)S(1)}) custom-call(s32[576]{0:T(1024)} %frag.3, s32[1,3]{1,0:T(1,128)} %delay.1, bf16[1,256,4608]{2,1,0:T(8,128)(2,1)} %residual.1, ...), custom_call_target="tpu_custom_call" | custom-call | tf_op jit(solution)/shard_map/inner_step/pallas_call | solution.py:641
  76.1 5.1 %update.1 = (f32[1,144,1024]{2,1,0:T(8,128)}, f32[1,144,1024]{2,1,0:T(8,128)}, f32[1,144,1024]{2,1,0:T(8,128)}, f32[144,1024]{1,0:T(8,128)}, f32[144,1024]{1,0:T...) custom-call(s32[576]{0:T(1024)} %frag.3, ...), custom_call_target="tpu_custom_call" | custom-call | tf_op jit(solution)/shard_map/update/pallas_call | solution.py:747

commit v4 on v3

--- a/solution.py
+++ b/solution.py
@@ -47,18 +47,18 @@
     ],
     [
         1, 5, 24, 0, 6, 2, 10, 4, 60, 8, 7, 11, 3, 14, 12, 61, 16, 78, 15, 37, 38, 9, 25, 13, 77, 79, 40, 39,
-        65, 50, 62, 63, 80, 49, 64, 74, 66, 67, 51, 83, 75, 81, 69, 82, 68, 41, 76, 28, 42, 26, 29, 84, 56,
-        57, 58, 30, 59, 17, 71, 70, 44, 43, 18, 73, 32, 31, 72, 20, 19, 27, 34, 45, 46, 47, 48, 33, 22, 21,
+        65, 50, 62, 63, 80, 49, 64, 74, 66, 67, 51, 83, 75, 81, 69, 82, 68, 41, 76, 28, 26, 29, 84, 56, 57,
+        42, 58, 30, 59, 17, 71, 70, 44, 43, 18, 73, 32, 31, 72, 20, 19, 27, 34, 45, 46, 47, 48, 33, 22, 21,
         23,
     ],
     [
-        14, 35, 15, 16, 36, 65, 60, 53, 40, 54, 67, 61, 37, 52, 66, 38, 55, 83, 78, 63, 69, 77, 81, 41, 62,
+        14, 35, 15, 16, 36, 65, 60, 53, 40, 54, 67, 61, 37, 52, 66, 38, 55, 83, 78, 63, 69, 77, 41, 81, 62,
         39, 24, 58, 68, 79, 82, 57, 49, 42, 80, 51, 84, 50, 43, 44, 56, 25, 71, 59, 64, 73, 74, 76, 45, 70,
         26, 29, 46, 75, 72, 47, 28, 30, 48, 32, 33, 27, 34, 31,
     ],
     [
-        14, 15, 16, 40, 41, 65, 66, 83, 84, 24, 35, 25, 57, 43, 69, 81, 36, 58, 82, 67, 68, 56, 38, 54, 60,
-        37, 59, 61, 71, 26, 73, 44, 55, 53, 39, 52, 27, 42, 63, 49, 62, 70, 77, 51, 50, 46, 72, 45, 64, 47,
+        14, 15, 16, 40, 41, 65, 66, 83, 84, 24, 35, 25, 57, 43, 69, 81, 36, 58, 82, 67, 68, 53, 56, 38, 54,
+        60, 37, 59, 61, 71, 26, 73, 44, 55, 39, 52, 27, 42, 63, 49, 62, 70, 77, 51, 50, 46, 72, 45, 64, 47,
         79, 48, 78, 80, 74, 76, 29, 75, 30, 32, 31, 28, 33, 34,
     ],
 ]
@@ -76,7 +76,7 @@
     opp, full, zbuf, zxbuf, oppx, fullx, oterm, obuf, osum, ozh, od,
     loc, part_s, part_r, agz_s, agz_r, agx_s, agx_r, axx_s, axx_r, axz_s, axz_r,
     rsx_s, rsx_r, rsz_s, rsz_r, rxz_s, rxz_r, rxx_s, rxx_r, gx_s, gx_r, gz_s, gz_r,
-    oy_s, oy_r, oz_s, oz_r, ob_s, ob_r,
+    oy_s, oy_r, oz_s, oz_r, ob_s, ob_r, ready_y, ready_z,
 ):
     me = lax.axis_index("fsdp")
     rep = lax.axis_index("replica")
@@ -133,10 +133,21 @@
     greeted = [partner]
     greeted += [dev(q, (x + k) % 4, c) for k in range(1, 4)]
     greeted += [dev((q + k) % 4, x, c) for k in range(1, 4)]
-    greeted += [{"replica": ((y + k) % 4) * 2 + zh} for k in range(1, 4)]
-    greeted += [{"replica": y * 2 + 1 - zh}]
     for to in greeted:
         pl.semaphore_signal(barrier, inc=1, device_id=to, device_id_type=MESH)
+
+    other_z = {"replica": y * 2 + 1 - zh}
+
+    @pl.when(zh == 0)
+    def _():
+        pl.semaphore_signal(barrier, inc=1, device_id=other_z, device_id_type=MESH)
+
+    for k in range(1, 4):
+        @pl.when(y + k < 4)
+        def _(k=k):
+            pl.semaphore_signal(
+                barrier, inc=1, device_id={"replica": (y + k) * 2 + zh}, device_id_type=MESH
+            )
 
     own = q % 2
     local_in[0].wait()
@@ -150,7 +161,18 @@
     def _():
         stage[...] = master_v[...].astype(BF16)
 
-    pl.semaphore_wait(barrier, len(greeted))
+    pl.semaphore_wait(barrier, len(greeted) + y + zh)
+
+    @pl.when(zh == 1)
+    def _():
+        pl.semaphore_signal(ready_z, inc=1, device_id=other_z, device_id_type=MESH)
+
+    for k in range(1, 4):
+        @pl.when(y >= k)
+        def _(k=k):
+            pl.semaphore_signal(
+                ready_y, inc=1, device_id={"replica": (y - k) * 2 + zh}, device_id_type=MESH
+            )
 
     zcols, xcols = pl.ds(0, NZ), pl.ds(NZ, NX)
 
@@ -418,6 +440,10 @@
                     taken = (delay[0, b] == k + 1).astype(F32)
                     term = term - taken * hist_v[k, spot, :]
                 oterm[spot, :] = term
+            @pl.when(y < 3)
+            def _():
+                pl.semaphore_wait(ready_y, 3 - y)
+
             obuf[y] = oterm[:, pl.ds(pl.multiple_of(y * QUART, 128), QUART)]
             for k in range(1, 4):
                 yy = (y + k) % 4
@@ -430,7 +456,11 @@
             for k in range(1, 4):
                 got(obuf.at[(y + 4 - k) % 4], oy_r.at[k])
             osum[...] = (obuf[0] + obuf[1]) + (obuf[2] + obuf[3])
-            go(osum, ozh, oz_s, oz_r, {"replica": y * 2 + 1 - zh})
+            @pl.when(zh == 0)
+            def _():
+                pl.semaphore_wait(ready_z, 1)
+
+            go(osum, ozh, oz_s, oz_r, other_z)
 
         def outer_last():
             got(ozh, oz_r)
@@ -637,6 +667,7 @@
         dma((2, 2, 4)), dma((2, 2, 4)), dma((6,)), dma((6,)),
         dma((4,)), dma((4,)), dma((4,)), dma((4,)),
         dma((4,)), dma((4,)), dma, dma, dma((4,)), dma((4,)),
+        pltpu.SemaphoreType.REGULAR, pltpu.SemaphoreType.REGULAR,
     ]
     return pl.pallas_call(
         main_kernel,

time: 81.6 us -> 79.2 us (0.971)
  Pallas kernels: 80.5 us -> 78.2 us
    pallas_call x1, Pallas kernels: 75.4 us -> 73.1 us  [main_call(): pl.pallas_call(main_kernel, out_shape=(jax.ShapeDtypeStruct((1, T, DV), B...]
where the time goes in v4:
time: 79.2 us; the launch traced here: 79 us
  Pallas kernels  78.2 us (99%)
  between operations  0.82 us (1%)
    pallas_call x1, Pallas kernels, main_call(): pl.pallas_call(main_kernel, out_shape=(jax.ShapeDtypeStruct((1, T, DV), B...  73.1 us
    pallas_call x1, Pallas kernels, update_call(): pl.pallas_call(update_kernel, out_shape=(like3, like3, like3, like2, like...  5.14 us

profile of v4, /device:TPU:1, one launch (start us, length us, event | category | flops | bytes accessed | tf_op | source)
XLA Modules:
  0.0 79.0 jit_solution(15251030755815995952)
XLA Ops:
  0.6 73.1 %inner_step.1 = (bf16[1,256,1024]{2,1,0:T(8,128)(2,1)S(1)}, bf16[1,256,4608]{2,1,0:T(8,128)(2,1)S(1)}, f32[1,4608]{1,0:T(1,128)S(1)}, bf16[144,1024]{1,0:T(8,128)(2,1)S(1)}, f32[24,1024]{1,0:T(8,128)S(1)}) custom-call(s32[576]{0:T(1024)} %frag.3, s32[1,3]{1,0:T(1,128)} %delay.1, bf16[1,256,4608]{2,1,0:T(8,128)(2,1)} %residual.1, ...), custom_call_target="tpu_custom_call" | custom-call | tf_op jit(solution)/shard_map/inner_step/pallas_call | solution.py:672
  73.7 5.1 %update.1 = (f32[1,144,1024]{2,1,0:T(8,128)}, f32[1,144,1024]{2,1,0:T(8,128)}, f32[1,144,1024]{2,1,0:T(8,128)}, f32[144,1024]{1,0:T(8,128)}, f32[144,1024]{1,0:T...) custom-call(s32[576]{0:T(1024)} %frag.3, ...), custom_call_target="tpu_custom_call" | custom-call | tf_op jit(solution)/shard_map/update/pallas_call | solution.py:778

commit v5 on v4

--- a/solution.py
+++ b/solution.py
@@ -69,8 +69,8 @@
 
 
 def main_kernel(
-    frag, delay, residual, cotangent, gain, master, anchor, history,
-    values_o, igrad_o, ggrad_o, grad_o, delta_o,
+    frag, delay, residual, cotangent, gain, master, anchor, history, first, second, momentum,
+    values_o, igrad_o, ggrad_o, grad_o, delta_o, master_c, first_c, second_c, anchor_c, momentum_c,
     res, resp, cot, gain_v, master_v, anchor_v, hist_v,
     wh, stage, g, normed, inv, dn, vacc, vrecv, vout, rs, rsp, ig, ggx, ggz, ggt,
     opp, full, zbuf, zxbuf, oppx, fullx, oterm, obuf, osum, ozh, od,
@@ -129,6 +129,14 @@
     for item in local_in:
         item.start()
 
+    carried = [
+        pltpu.make_async_copy(src, dst, loc.at[12 + k])
+        for k, (src, dst) in enumerate((
+            (master.at[0], master_c), (first.at[0], first_c), (second.at[0], second_c),
+            (anchor, anchor_c), (momentum, momentum_c),
+        ))
+    ]
+
     barrier = pltpu.get_barrier_semaphore()
     greeted = [partner]
     greeted += [dev(q, (x + k) % 4, c) for k in range(1, 4)]
@@ -194,6 +202,9 @@
     go(cotangent.at[0], cot.at[pl.ds(T, T)], part_s.at[2], part_r.at[2], partner)
 
     first_sends = len(sends)
+
+    for item in carried:
+        item.start()
 
     def all_steps(owner, order):
         def slot_of(k):
@@ -640,11 +651,13 @@
         def _(owner=kind < 2, order=order):
             all_steps(owner, order)
 
+    for item in carried:
+        item.wait()
     for cond, made in sends:
         when(cond, lambda made=made: made.wait_send())
 
 
-def main_call(frag, delay, residual, cotangent, gain, master, anchor, history):
+def main_call(frag, delay, residual, cotangent, gain, master, anchor, history, first, second, momentum):
     any_space = pl.BlockSpec(memory_space=pl.ANY)
     smem = pl.BlockSpec(memory_space=pltpu.SMEM)
     vm = pltpu.VMEM
@@ -661,7 +674,7 @@
         vm((2, 2, 4, SLOT, nx), BF16), vm((2, R, nx), BF16), vm((2, SLOT, nx), BF16),
         vm((PART, DV), F32), vm((4, PART, QUART), F32), vm((PART, QUART), F32),
         vm((PART, QUART), F32), vm((PART, DV), F32),
-        dma((12,)), dma((10,)), dma((10,)), dma((2, 2, 2)), dma((2, 2)), dma((2, 6)), dma((2, 6)),
+        dma((17,)), dma((10,)), dma((10,)), dma((2, 2, 2)), dma((2, 2)), dma((2, 6)), dma((2, 6)),
         dma((6,)), dma((6,)), dma((2, 4, 2)), dma((2, 4)),
         dma((2, 6)), dma((2, 6)), dma((2, 2, 2)), dma((2, 2, 2)),
         dma((2, 2, 4)), dma((2, 2, 4)), dma((6,)), dma((6,)),
@@ -677,59 +690,34 @@
             jax.ShapeDtypeStruct((1, D), F32),
             jax.ShapeDtypeStruct((R, DV), BF16),
             jax.ShapeDtypeStruct((PART, DV), F32),
-        ),
-        in_specs=[smem, smem] + [any_space] * 6,
-        out_specs=(any_space,) * 5,
+        ) + (jax.ShapeDtypeStruct((R, DV), F32),) * 5,
+        in_specs=[smem, smem] + [any_space] * 9,
+        out_specs=(any_space,) * 10,
         scratch_shapes=scratch,
         compiler_params=pltpu.CompilerParams(
             collective_id=0, has_side_effects=True, vmem_limit_bytes=44 * 1024 * 1024
         ),
         name="inner_step",
-    )(frag, delay, residual, cotangent, gain, master, anchor, history)
+    )(frag, delay, residual, cotangent, gain, master, anchor, history, first, second, momentum)
 
 
 def update_kernel(
-    frag, grad, delta, master, first, second, anchor, momentum, values, igrad, ggrad,
+    frag, grad_v, delta_v, master_v, first_v, second_v, anchor_v, momentum_v, values, igrad, ggrad,
     master_o, first_o, second_o, anchor_o, momentum_o, values_o, igrad_o, ggrad_o,
-    grad_v, delta_v, master_v, first_v, second_v, anchor_v, momentum_v,
-    master_n, first_n, second_n, load, load_small, stored, through,
+    master_n, first_n, second_n, anchor_n, momentum_n, stored, through,
 ):
     rows = FRAGS * FR_ROWS
     groups = R // rows
     spots = [pl.ds(i * rows, rows) for i in range(groups)]
-    small = [
-        pltpu.make_async_copy(grad, grad_v, load_small.at[0]),
-        pltpu.make_async_copy(delta, delta_v, load_small.at[1]),
-    ]
-    for item in small:
-        item.start()
-    loads = []
-    for i, at in enumerate(spots):
-        loads.append([
-            pltpu.make_async_copy(src, dst, load.at[i, k])
-            for k, (src, dst) in enumerate((
-                (master.at[0, at], master_v.at[at]),
-                (first.at[0, at], first_v.at[at]),
-                (second.at[0, at], second_v.at[at]),
-                (anchor.at[at], anchor_v.at[at]),
-                (momentum.at[at], momentum_v.at[at]),
-            ))
-        ])
-    for item in loads[0] + loads[1] + loads[2]:
-        item.start()
     passed = [
         pltpu.make_async_copy(src, dst, through.at[k])
         for k, (src, dst) in enumerate(((igrad, igrad_o), (values, values_o), (ggrad, ggrad_o)))
     ]
     for item in passed:
         item.start()
-    for item in small:
-        item.wait()
     begin = lax.axis_index("fsdp") * (R // FR_ROWS)
     stores = []
     for i, at in enumerate(spots):
-        for item in loads[i]:
-            item.wait()
         chosen = jnp.int32(0)
         for k in range(1, FRAGS):
             chosen = chosen + jnp.where(frag[begin + i * FRAGS + k] == 0, k, 0)
@@ -739,16 +727,18 @@
         anchor_old = anchor_v[block, :]
         momentum_part = outer_beta * momentum_v[block, :] + change
         anchor_part = anchor_old - outer_rate * (change + outer_beta * momentum_part)
-        anchor_v[block, :] = anchor_part
-        momentum_v[block, :] = momentum_part
+        anchor_n[at, :] = anchor_v[at, :]
+        momentum_n[at, :] = momentum_v[at, :]
+        anchor_n[block, :] = anchor_part
+        momentum_n[block, :] = momentum_part
 
         def store(k, src, dst):
             item = pltpu.make_async_copy(src, dst, stored.at[i, k])
             item.start()
             stores.append(item)
 
-        store(0, anchor_v.at[at], anchor_o.at[at])
-        store(1, momentum_v.at[at], momentum_o.at[at])
+        store(0, anchor_n.at[at], anchor_o.at[at])
+        store(1, momentum_n.at[at], momentum_o.at[at])
         for piece in range(rows // 16):
             part = pl.ds(i * rows + piece * 16, 16)
             gradient = grad_v[part, :].astype(F32)
@@ -783,11 +773,11 @@
             jax.ShapeDtypeStruct((1, T, D), BF16),
             jax.ShapeDtypeStruct((1, D), F32),
         ),
-        in_specs=[pl.BlockSpec(memory_space=pltpu.SMEM)] + [any_space] * 10,
+        in_specs=[pl.BlockSpec(memory_space=pltpu.SMEM)]
+        + [pl.BlockSpec(memory_space=pltpu.VMEM)] * 7
+        + [any_space] * 3,
         out_specs=(any_space,) * 8,
-        scratch_shapes=[pltpu.VMEM((R, DV), BF16), pltpu.VMEM((PART, DV), F32)]
-        + [whole] * 8
-        + [dma((groups, 5)), dma((2,)), dma((groups, 5)), dma((3,))],
+        scratch_shapes=[whole] * 5 + [dma((groups, 5)), dma((3,))],
         compiler_params=pltpu.CompilerParams(vmem_limit_bytes=16 * 1024 * 1024),
         name="update",
     )(frag, grad, delta, master, first, second, anchor, momentum, values, igrad, ggrad)
@@ -807,11 +797,12 @@
             anchor, outer_momentum, history, fragment, delay,
         )
     ]
-    values, input_grad, gain_grad, gradient, delta = main_call(
-        fragment, delay, residual, cotangent, norm_gain, master, anchor, history
+    values, input_grad, gain_grad, gradient, delta, *carried = main_call(
+        fragment, delay, residual, cotangent, norm_gain, master, anchor, history,
+        first_moment, second_moment, outer_momentum,
     )
     new_master, new_first, new_second, new_anchor, new_momentum, values, input_grad, gain_grad = update_call(
-        fragment, gradient, delta, master, first_moment, second_moment, anchor, outer_momentum,
+        fragment, gradient, delta, *carried,
         values, input_grad, gain_grad,
     )
     return (

time: 79.2 us -> 77.5 us (0.979)
  Pallas kernels: 78.2 us -> 76.5 us
    pallas_call x1, Pallas kernels: 5.14 us -> 3.41 us  [update_call(): pl.pallas_call(update_kernel, out_shape=(like3, like3, like3, like2, like...]
where the time goes in v5:
time: 77.5 us; the launch traced here: 77.4 us
  Pallas kernels  76.5 us (99%)
  between operations  0.83 us (1%)
    pallas_call x1, Pallas kernels, main_call(): pl.pallas_call(main_kernel, out_shape=(jax.ShapeDtypeStruct((1, T, DV), B...  73.1 us
    pallas_call x1, Pallas kernels, update_call(): pl.pallas_call(update_kernel, out_shape=(like3, like3, like3, like2, like...  3.41 us

profile of v5, /device:TPU:1, one launch (start us, length us, event | category | flops | bytes accessed | tf_op | source)
XLA Modules:
  0.0 77.4 jit_solution(10080921642421299588)
XLA Ops:
  0.6 73.1 %inner_step.1 = (bf16[1,256,1024]{2,1,0:T(8,128)(2,1)S(1)}, bf16[1,256,4608]{2,1,0:T(8,128)(2,1)S(1)}, f32[1,4608]{1,0:T(1,128)S(1)}, bf16[144,1024]{1,0:T(8,128...) custom-call(s32[576]{0:T(1024)} %frag.3, ...), custom_call_target="tpu_custom_call" | custom-call | tf_op jit(solution)/shard_map/inner_step/pallas_call | solution.py:685
  73.8 3.4 %update.1 = (f32[1,144,1024]{2,1,0:T(8,128)}, f32[1,144,1024]{2,1,0:T(8,128)}, f32[1,144,1024]{2,1,0:T(8,128)}, f32[144,1024]{1,0:T(8,128)}, f32[144,1024]{1,0:T...) custom-call(s32[576]{0:T(1024)} %frag.3, ...), custom_call_target="tpu_custom_call" | custom-call | tf_op jit(solution)/shard_map/update/pallas_call | solution.py:768
